TPU v7x, 128 devices: a whole 4x4x4 slice. The times are simulated.
128 devices in a mesh: wide: 16 (over x, y), narrow: 8 (over z, core).
Axes of the slice: x: 4, y: 4, z: 4, core: 2. Of those that a mesh axis runs over, the one named last changes fastest.
Arguments:
- classes: float32 [32, 256, 128, 128], P(None, 'wide', 'narrow'), may hold values from 0.1 to 2
- velocity: float32 [3, 256, 128, 128], P(None, 'wide', 'narrow'), may hold values from -0.3 to 0.3
- attach_rate: float32 [32], replicated, may hold values from 0.05 to 1
- bubble_pos: float32 [12288, 3, 128], P(('wide', 'narrow')), may hold values from 0 to 1
- bubble_volume: float32 [12288, 128], P(('wide', 'narrow')), may hold values from 0.05 to 0.5
- bubble_area: float32 [12288, 128], P(('wide', 'narrow')), may hold values from 0.2 to 2
- bubble_count: int32 [1536, 8], P(('wide', 'narrow')), may hold values from 1 to 128, 640 in all within a row
- cluster_target: int32 [12288, 1], P(('wide', 'narrow')), may hold values from 0 to 127; in each aligned block of 96 rows (0 to 95, 96 to 191, ...) at most 2 rows name the same one
- cluster_offset: int32 [12288, 2], P(('wide', 'narrow')), may hold values from 0 to 12
Outputs:
- deposit: float32 [2, 256, 128, 128], P(None, 'wide', 'narrow')
- transported: float32 [32, 256, 128, 128], P(None, 'wide', 'narrow')
Inputs may be any that keep to these rules, and one draw needn't show every extreme that they name: `cluster_target`: within the clusters listed on one device no brick is named more than 2 times, a bound that some block reaches. `bubble_count`: the counts of each row of 8 sum to 640; some cluster of each row is full.
All inputs are finite; a program needn't handle non-finite values.
Results may differ from a plain program's by a relative error of at most 0.0001.
Values sent between devices are 32-bit elements; how exact they have to be, the bound alone decides.
No kernel may reach another device: no remote copies, remote signals or barrier semaphores. Data moves between devices by JAX's collectives and lax.ppermute only.
A program may use at most 128 MiB of HBM per device.

v0:
```python
import functools

import jax
import jax.numpy as jnp
from jax import lax
from jax.experimental import pallas as pl
from jax.experimental.pallas import tpu as pltpu
from jax.sharding import PartitionSpec as P

WIN = 4
DEPTH = 4
GROUP = 8
AXES = ("wide", "narrow")
VMEM_BYTES = 60 * 1024 * 1024

CORNER = [(a, b) for a in range(DEPTH - 1) for b in range(DEPTH - 1 - a)]


def params(**more):
    return pltpu.CompilerParams(vmem_limit_bytes=VMEM_BYTES, **more)


def rolled(block, wide_step, narrow_step):
    wide_count, narrow_count = lax.axis_size("wide"), lax.axis_size("narrow")
    pairs = [
        (
            w * narrow_count + n,
            (w + wide_step) % wide_count * narrow_count + (n + narrow_step) % narrow_count,
        )
        for w in range(wide_count)
        for n in range(narrow_count)
    ]
    return lax.ppermute(block, AXES, pairs)


def pack_kernel(meta, pos, volume, area, sent, tally):
    clusters, _, bubbles = pos.shape
    devices = sent.shape[0]
    sent[...] = jnp.zeros_like(sent)

    def clear(d, carry):
        tally[d] = 0
        return carry

    lax.fori_loop(0, devices, clear, 0)
    lane = lax.broadcasted_iota(jnp.int32, (1, bubbles), 1)

    def one(c, carry):
        target, count = meta[c], meta[clusters + c]
        corner_x = meta[2 * clusters + c].astype(jnp.float32)
        corner_y = meta[3 * clusters + c].astype(jnp.float32)
        rank = tally[target]
        tally[target] = rank + 1
        base = rank * (5 * bubbles)
        live = lane < count
        rows = [
            pos[c, 0:1, :] * 4.0,
            pos[c, 1:2, :] * 4.0,
            pos[c, 2:3, :] * 128.0,
            jnp.where(live, volume[pl.ds(c, 1), :], 0.0),
            jnp.where(live, area[pl.ds(c, 1), :], 0.0),
        ]
        for i, row in enumerate(rows):
            start = pl.multiple_of(base + i * bubbles, bubbles)
            sent[target, :, pl.ds(start, bubbles)] = row
        tail = sent[target, :, pl.ds(10 * bubbles, bubbles)]
        tail = jnp.where(lane == 2 * rank, corner_x, tail)
        tail = jnp.where(lane == 2 * rank + 1, corner_y, tail)
        sent[target, :, pl.ds(10 * bubbles, bubbles)] = tail
        return carry

    lax.fori_loop(0, clusters, one, 0, unroll=4)


def pack(meta, pos, volume, area, devices):
    bubbles = pos.shape[2]
    return pl.pallas_call(
        pack_kernel,
        out_shape=jax.ShapeDtypeStruct((devices, 1, 11 * bubbles), jnp.float32),
        in_specs=[pl.BlockSpec(memory_space=pltpu.SMEM)]
        + [pl.BlockSpec(memory_space=pltpu.VMEM)] * 3,
        out_specs=pl.BlockSpec(memory_space=pltpu.VMEM),
        scratch_shapes=[pltpu.SMEM((devices,), jnp.int32)],
        compiler_params=params(),
    )(meta, pos, volume, area)


UNROLL = 4


def halves(value):
    high = value.astype(jnp.bfloat16)
    return high, (value - high.astype(jnp.float32)).astype(jnp.bfloat16)


def across(left, right):
    return lax.dot_general(
        left, right, (((1,), (1,)), ((), ())), preferred_element_type=jnp.float32
    )


def bell(distance):
    return jnp.exp2((distance * (-0.5 * 1.4426950408889634)) * distance)


def deposit_kernel(got_any, got, deposit, attach, total, corners, sem):
    devices = got.shape[0]
    bubbles = got.shape[2] // 11
    copy = pltpu.make_async_copy(
        got_any.at[:, :, pl.ds(10 * bubbles, bubbles)], corners, sem
    )
    copy.start()
    total[...] = jnp.zeros_like(total)
    copy.wait()
    row = lax.broadcasted_iota(jnp.int32, (8, bubbles), 0)
    is_volume = row % 2 == 0
    cell_y = (row // 2).astype(jnp.float32) + 0.5
    cell_z = lax.broadcasted_iota(jnp.int32, (128, bubbles), 0).astype(jnp.float32) + 0.5

    def sources(step, carry):
        done = []
        for u in range(UNROLL):
            for slot in range(2):
                source = step * UNROLL + u
                px, py, pz, vol, are = (
                    got[source, :, (5 * slot + i) * bubbles : (5 * slot + i + 1) * bubbles]
                    for i in range(5)
                )
                share = bell(cell_y - py) * jnp.where(is_volume, vol, are)
                plane = jnp.concatenate(
                    [share * bell((i + 0.5) - px) for i in range(WIN)], axis=0
                )
                plane_high, plane_low = halves(plane)
                high, low = halves(bell(cell_z - pz))
                both = across(jnp.concatenate([plane_high, plane_low], axis=0), high)
                window = both[:32] + both[32:] + across(plane_high, low)
                done.append((source, slot, window))
        for source, slot, window in done:
            x = corners[source, 0, 2 * slot].astype(jnp.int32)
            y = corners[source, 0, 2 * slot + 1].astype(jnp.int32)
            for i in range(WIN):
                at = pl.ds((x + i) * 32 + y * 2, 8)
                total[at, :] = total[at, :] + window[8 * i : 8 * i + 8]
        return carry

    lax.fori_loop(0, devices // UNROLL, sources, 0)
    for x in range(16):
        gas = total[pl.ds(x * 32, 16, stride=2), :]
        face = total[pl.ds(x * 32 + 1, 16, stride=2), :]
        deposit[0, x] = gas
        deposit[1, x] = face
        attach[x] = face / (1.0 + gas)


def deposited(got):
    devices = got.shape[0]
    return pl.pallas_call(
        deposit_kernel,
        out_shape=(
            jax.ShapeDtypeStruct((2, 16, 16, 128), jnp.float32),
            jax.ShapeDtypeStruct((16, 16, 128), jnp.float32),
        ),
        in_specs=[
            pl.BlockSpec(memory_space=pl.ANY),
            pl.BlockSpec(memory_space=pltpu.VMEM),
        ],
        out_specs=(pl.BlockSpec(memory_space=pltpu.VMEM),) * 2,
        scratch_shapes=[
            pltpu.VMEM((512, 128), jnp.float32),
            pltpu.SMEM((devices, 1, 128), jnp.float32),
            pltpu.SemaphoreType.DMA,
        ],
        compiler_params=params(),
    )(got, got)


WIDE_ROWS = 16 * 32 + 3 * 16
SIDE_ROWS = DEPTH * 32 + 16
CORNER_ROWS = len(CORNER) * 32 + 24


def strips_kernel(classes, velocity, own, wide_low, wide_high, side_low, side_high, *corners):
    x = pl.program_id(0)
    cells = jnp.swapaxes(classes[:, 0], 0, 1)
    speed = velocity[:, 0]
    flat = cells.reshape(16 * 32, 128)
    own[0] = flat

    @pl.when(x < DEPTH)
    def _():
        wide_low[0, 0:512, :] = flat
        wide_low[0, 512:560, :] = speed.reshape(48, 128)

    @pl.when(x >= 16 - DEPTH)
    def _():
        wide_high[0, 0:512, :] = flat
        wide_high[0, 512:560, :] = speed.reshape(48, 128)

    for out, first in ((side_low, 0), (side_high, 16 - DEPTH)):
        out[0, 0:128, :] = flat[first * 32 : (first + DEPTH) * 32]
        for d in range(3):
            out[0, 128 + 4 * d : 132 + 4 * d, :] = speed[d, first : first + DEPTH]
    for at, out in enumerate(corners):
        high_x, high_y = divmod(at, 2)
        for a in range(DEPTH - 1):

            @pl.when(x == (15 - a if high_x else a))
            def _(a=a, high_x=high_x, high_y=high_y, out=out):
                for cell, (this_a, b) in enumerate(CORNER):
                    if this_a == a:
                        y = 15 - b if high_y else b
                        out[cell * 32 : cell * 32 + 32, :] = flat[y * 32 : y * 32 + 32]
                        for d in range(3):
                            at_row = len(CORNER) * 32 + 3 * cell + d
                            out[at_row : at_row + 1, :] = speed[d, y : y + 1]


def strips(classes, velocity):
    def rows(*count):
        return jax.ShapeDtypeStruct(count + (128,), jnp.float32)

    return pl.pallas_call(
        strips_kernel,
        grid=(16,),
        out_shape=(rows(16, 512),)
        + (rows(DEPTH, WIDE_ROWS),) * 2
        + (rows(16, SIDE_ROWS),) * 2
        + (rows(CORNER_ROWS),) * 4,
        in_specs=[
            pl.BlockSpec((32, 1, 16, 128), lambda x: (0, x, 0, 0)),
            pl.BlockSpec((3, 1, 16, 128), lambda x: (0, x, 0, 0)),
        ],
        out_specs=(
            pl.BlockSpec((1, 512, 128), lambda x: (x, 0, 0)),
            pl.BlockSpec((1, WIDE_ROWS, 128), lambda x: (jnp.minimum(x, DEPTH - 1), 0, 0)),
            pl.BlockSpec((1, WIDE_ROWS, 128), lambda x: (jnp.maximum(x - 16 + DEPTH, 0), 0, 0)),
            pl.BlockSpec((1, SIDE_ROWS, 128), lambda x: (x, 0, 0)),
            pl.BlockSpec((1, SIDE_ROWS, 128), lambda x: (x, 0, 0)),
        )
        + (pl.BlockSpec((CORNER_ROWS, 128), lambda x: (0, 0)),) * 4,
        compiler_params=params(),
    )(classes, velocity)


SPAN = 16 + 2 * DEPTH
ORIGIN = 8


def transport_kernel(
    own, wide_low, wide_high, side_low, side_high, c00, c01, c10, c11,
    velocity, attach, attach_low, attach_high, rate,
    out,
    field, other, factor, speed, coef, side_speed, corner_buf, stage,
    sem, out_sem,
):
    corners = (c00, c01, c10, c11)
    copies = []

    def copy(source, target):
        moved = pltpu.make_async_copy(source, target, sem.at[len(copies)])
        moved.start()
        copies.append(moved)

    inner = pl.ds(DEPTH, 16)
    copy(velocity, speed.at[:, inner, pl.ds(ORIGIN, 16)])
    for side, block in enumerate((side_low, side_high)):
        copy(block.at[:, pl.ds(DEPTH * 32, 16)], side_speed.at[side])
    for at, block in enumerate(corners):
        copy(block, corner_buf.at[at])
    for block, first in ((wide_low, 0), (wide_high, 16 + DEPTH)):
        for d in range(3):
            copy(
                block.at[:, pl.ds(512 + 16 * d, 16)],
                speed.at[d, pl.ds(first, DEPTH), pl.ds(ORIGIN, 16)],
            )
    for block, first in ((wide_low, 0), (wide_high, 16 + DEPTH)):
        copy(
            block.at[:, pl.ds(0, 512)],
            field.at[pl.ds(first, DEPTH), pl.ds(DEPTH * 32, 512)],
        )
    for block, first in ((side_low, 0), (side_high, 16 + DEPTH)):
        copy(block.at[:, pl.ds(0, DEPTH * 32)], field.at[inner, pl.ds(first * 32, DEPTH * 32)])
    copy(own, field.at[inner, pl.ds(DEPTH * 32, 512)])
    for moved in copies:
        moved.wait()

    for side, first in ((0, ORIGIN - DEPTH), (1, ORIGIN + 16)):
        for x in range(16):
            for d in range(3):
                speed[d, DEPTH + x, first : first + DEPTH, :] = side_speed[
                    side, x, 4 * d : 4 * d + 4, :
                ]
    for at in range(4):
        high_x, high_y = divmod(at, 2)
        for cell, (a, b) in enumerate(CORNER):
            x = 16 + DEPTH + a if high_x else DEPTH - 1 - a
            y = 16 + DEPTH + b if high_y else DEPTH - 1 - b
            field[x, y * 32 : y * 32 + 32, :] = corner_buf[at, cell * 32 : cell * 32 + 32, :]
            yv = y + ORIGIN - DEPTH
            for d in range(3):
                at_row = len(CORNER) * 32 + 3 * cell + d
                speed[d, x, yv : yv + 1, :] = corner_buf[at, at_row : at_row + 1, :]

    wide_at, narrow_at = lax.axis_index("wide"), lax.axis_index("narrow")
    wide_last, narrow_last = lax.axis_size("wide") - 1, lax.axis_size("narrow") - 1
    edges = (wide_at == 0, wide_at == wide_last, narrow_at == 0, narrow_at == narrow_last)
    spans = ((0, DEPTH), (16 + DEPTH, SPAN))

    def clear(ref, by_rows):
        for side, (first, last) in enumerate(spans):

            @pl.when(edges[side])
            def _(first=first, last=last):
                ref[first:last] = jnp.zeros((last - first,) + ref.shape[1:], jnp.float32)

            @pl.when(edges[2 + side])
            def _(first=first, last=last):
                ref[:, first * by_rows : last * by_rows] = jnp.zeros(
                    (ref.shape[0], (last - first) * by_rows, 128), jnp.float32
                )

    clear(field, 32)
    for side, (first, last) in enumerate(spans):

        @pl.when(edges[side])
        def _(first=first, last=last):
            speed[:, first:last] = jnp.zeros((3, last - first) + speed.shape[2:], jnp.float32)

        @pl.when(edges[2 + side])
        def _(first=first, last=last):
            shift = ORIGIN - DEPTH
            speed[:, :, first + shift : last + shift] = jnp.zeros(
                (3, SPAN, last - first, 128), jnp.float32
            )

    lane = lax.broadcasted_iota(jnp.int32, (SPAN - 2, 128), 1)

    def coefficients(x, carry):
        low, high = ORIGIN - DEPTH + 1, ORIGIN + 16 + DEPTH - 1

        def at(d, dx, dy):
            return speed[d, x + dx, low + dy : high + dy, :]

        middle = [at(d, 0, 0) for d in range(3)]
        left = 0.5 * (at(0, -1, 0) + middle[0])
        right = 0.5 * (middle[0] + at(0, 1, 0))
        kept = 1.0 - jnp.maximum(right, 0.0) + jnp.minimum(left, 0.0)
        coef[1, x, low:high, :] = jnp.maximum(left, 0.0)
        coef[2, x, low:high, :] = -jnp.minimum(right, 0.0)
        left = 0.5 * (at(1, 0, -1) + middle[1])
        right = 0.5 * (middle[1] + at(1, 0, 1))
        kept = kept - jnp.maximum(right, 0.0) + jnp.minimum(left, 0.0)
        coef[3, x, low:high, :] = jnp.maximum(left, 0.0)
        coef[4, x, low:high, :] = -jnp.minimum(right, 0.0)
        before = jnp.where(lane == 0, 0.0, pltpu.roll(middle[2], 1, 1))
        after = jnp.where(lane == 127, 0.0, pltpu.roll(middle[2], 127, 1))
        left, right = 0.5 * (before + middle[2]), 0.5 * (middle[2] + after)
        kept = kept - jnp.maximum(right, 0.0) + jnp.minimum(left, 0.0)
        coef[5, x, low:high, :] = jnp.where(lane == 0, 0.0, jnp.maximum(left, 0.0))
        coef[6, x, low:high, :] = jnp.where(lane == 127, 0.0, -jnp.minimum(right, 0.0))
        coef[0, x, low:high, :] = kept
        return carry

    lax.fori_loop(1, SPAN - 1, coefficients, 0)

    groups = 32 // GROUP
    rates = [-rate[g * GROUP : (g + 1) * GROUP, :] for g in range(groups)]

    def row_of_step(step, reach, x, source, target, live):
        def cell(dx, y, g):
            return source[x + dx, y * 32 + g * GROUP : y * 32 + (g + 1) * GROUP, :]

        first, last = DEPTH - reach, DEPTH + 16 + reach
        before = [cell(0, first - 1, g) for g in range(groups)]
        now = [cell(0, first, g) for g in range(groups)]
        done = []
        for y in range(first, last):
            after = [cell(0, y + 1, g) for g in range(groups)]
            yv = y + ORIGIN - DEPTH
            k = [
                jnp.broadcast_to(coef[i, x, yv : yv + 1, :], (GROUP, 128)) for i in range(7)
            ]
            if step == 0:
                if y < DEPTH:
                    load = attach_low[x - 1, y - 1 : y, :]
                elif y < DEPTH + 16:
                    load = attach[x - 1, y - DEPTH : y - DEPTH + 1, :]
                else:
                    load = attach_high[x - 1, y - DEPTH - 16 : y - DEPTH - 15, :]
                kill = live
                if y < DEPTH:
                    kill = kill & ~edges[2]
                elif y >= DEPTH + 16:
                    kill = kill & ~edges[3]
                kill = kill.astype(jnp.float32)
            for g in range(groups):
                value = k[0] * now[g]
                value = value + k[1] * cell(-1, y, g)
                value = value + k[2] * cell(1, y, g)
                value = value + k[3] * before[g]
                value = value + k[4] * after[g]
                value = value + k[5] * pltpu.roll(now[g], 1, 1)
                value = value + k[6] * pltpu.roll(now[g], 127, 1)
                rows = slice(y * 32 + g * GROUP, y * 32 + (g + 1) * GROUP)
                if step == 0:
                    scale = jnp.exp(rates[g] * load) * kill
                    factor[x, rows, :] = scale
                else:
                    scale = factor[x, rows, :]
                value = value * scale
                if target is None:
                    done.append(value)
                else:
                    target[x, rows, :] = value
            before, now = now, after
        return done

    source, target = field, other
    for step in range(DEPTH):
        reach = DEPTH - 1 - step
        if step < DEPTH - 1:

            def middle_rows(i, carry, step=step, reach=reach, source=source, target=target):
                row_of_step(step, reach, DEPTH + i, source, target, jnp.bool_(True))
                return carry

            lax.fori_loop(0, 16, middle_rows, 0)
            for away in range(1, reach + 1):

                def outer(i, carry, away=away, step=step, reach=reach, source=source, target=target):
                    x = DEPTH - away + i * (15 + 2 * away)
                    live = jnp.where(i == 0, wide_at != 0, wide_at != wide_last)
                    row_of_step(step, reach - away, x, source, target, live)
                    return carry

                lax.fori_loop(0, 2, outer, 0)
        else:

            def last_rows(i, carry, step=step, source=source):
                done = row_of_step(step, 0, DEPTH + i, source, None, None)
                row = jnp.concatenate(done, axis=0).reshape(16, 32, 128)
                stage[:, i] = jnp.swapaxes(row, 0, 1)
                pltpu.make_async_copy(stage.at[:, i], out.at[:, i], out_sem).start()
                return carry

            lax.fori_loop(0, 16, last_rows, 0)
            pltpu.make_async_copy(stage, out, out_sem).wait()
        source, target = target, source


def transported(own, halos, velocity, attach, attach_low, attach_high, rate):
    vmem = pl.BlockSpec(memory_space=pltpu.VMEM)
    anywhere = pl.BlockSpec(memory_space=pl.ANY)
    return pl.pallas_call(
        transport_kernel,
        out_shape=jax.ShapeDtypeStruct((32, 16, 16, 128), jnp.float32),
        in_specs=[anywhere] * 10 + [vmem] * 4,
        out_specs=anywhere,
        scratch_shapes=[
            pltpu.VMEM((SPAN, SPAN * 32, 128), jnp.float32),
            pltpu.VMEM((SPAN, SPAN * 32, 128), jnp.float32),
            pltpu.VMEM((SPAN, SPAN * 32, 128), jnp.float32),
            pltpu.VMEM((3, SPAN, 32, 128), jnp.float32),
            pltpu.VMEM((7, SPAN, 32, 128), jnp.float32),
            pltpu.VMEM((2, 16, 16, 128), jnp.float32),
            pltpu.VMEM((4, CORNER_ROWS, 128), jnp.float32),
            pltpu.VMEM((32, 16, 16, 128), jnp.float32),
            pltpu.SemaphoreType.DMA((18,)),
            pltpu.SemaphoreType.DMA,
        ],
        compiler_params=params(),
    )(own, *halos, velocity, attach, attach_low, attach_high, rate)


def body(
    classes,
    velocity,
    attach_rate,
    bubble_pos,
    bubble_volume,
    bubble_area,
    bubble_count,
    cluster_target,
    cluster_offset,
):
    devices = lax.axis_size("wide") * lax.axis_size("narrow")
    meta = jnp.concatenate(
        [
            cluster_target.reshape(-1),
            bubble_count.reshape(-1),
            cluster_offset[:, 0],
            cluster_offset[:, 1],
        ]
    )
    sent = pack(meta, bubble_pos, bubble_volume, bubble_area, devices)
    got = lax.all_to_all(sent, AXES, split_axis=0, concat_axis=0, tiled=True)

    own, wide_low, wide_high, side_low, side_high, *corners = strips(classes, velocity)
    steps = ((1, 1), (1, -1), (-1, 1), (-1, -1))
    c00 = rolled(corners[3], *steps[0])
    c01 = rolled(corners[2], *steps[1])
    c10 = rolled(corners[1], *steps[2])
    c11 = rolled(corners[0], *steps[3])
    halos = (
        rolled(wide_high, 1, 0),
        rolled(wide_low, -1, 0),
        rolled(side_high, 0, 1),
        rolled(side_low, 0, -1),
        c00,
        c01,
        c10,
        c11,
    )
    deposit, attach = deposited(got)
    reach = DEPTH - 1
    tall = jnp.concatenate(
        [rolled(attach[-reach:], 1, 0), attach, rolled(attach[:reach], -1, 0)], axis=0
    )
    attach_low = rolled(tall[:, -reach:], 0, 1)
    attach_high = rolled(tall[:, :reach], 0, -1)
    rate = jnp.broadcast_to(attach_rate[:, None], (32, 128))
    return deposit, transported(
        own, halos, velocity, tall, attach_low, attach_high, rate
    )


def solution(mesh):
    return jax.shard_map(
        body,
        mesh=mesh,
        in_specs=(
            P(None, "wide", "narrow", None),
            P(None, "wide", "narrow", None),
            P(),
            P(("wide", "narrow"), None, None),
            P(("wide", "narrow"), None),
            P(("wide", "narrow"), None),
            P(("wide", "narrow"), None),
            P(("wide", "narrow"), None),
            P(("wide", "narrow"), None),
        ),
        out_specs=(P(None, "wide", "narrow", None), P(None, "wide", "narrow", None)),
        check_vma=False,
    )
```

profile of v0, /device:TPU:0, one launch (start us, length us, event | category | flops | bytes accessed | tf_op | source)
XLA Modules:
  0.0 136.7 jit_solution(14894117611356899354)
XLA Ops:
  0.6 0.8 slice_bitcast_fusion.1
  1.4 0.8 copy.13
  2.2 0.1 reshape.12
  2.2 1.7 %copy.14.pos = f32[96,3,128]{2,1,0:T(4,128)} copy(f32[96,3,128]{2,0,1:T(8,128)} %param.12) | data formatting | bytes 294912 | tf_op args[3]
  3.9 1.3 pad_add_fusion.meta
  5.2 3.9 %shard_map.104 = f32[128,1,1408]{2,1,0:T(1,128)} custom-call(s32[384]{0:T(512)} %pad_add_fusion.meta, f32[96,3,128]{2,1,0:T(4,128)} %copy.14.pos, f32[96,128]{1,0:T(8,128)} %volume.1, f32[96,128]{1,0:T(8,128)} %area.1), custom_call_target="tpu_custom_call" | custom-call | tf_op jit(solution)/shard_map/pallas_call | solution.py:77
  9.1 11.1 %all-to-all-start = ((f32[128,1,1408]{2,1,0:T(1,128)}), f32[128,1,1408]{2,1,0:T(1,128)S(1)}, u32[]{:S(2)}, u32[]{:S(2)}) async-start(f32[128,1,1408]{2,1,0:T(1,128)} %shard_map.104), calls=%async_computation | async-start | bytes 1441792 | tf_op jit(solution)/shard_map/all_to_all | solution.py:496
  20.3 11.9 %shard_map.106 = (f32[16,512,128]{2,1,0:T(8,128)}, f32[4,560,128]{2,1,0:T(8,128)}, f32[4,560,128]{2,1,0:T(8,128)}, f32[16,144,128]{2,1,0:T(8,128)}, f32[16,144,1...) custom-call(f32[32,16,16,128]{3,2,1,0:T(8,128)} %classes.1, ...), custom_call_target="tpu_custom_call" | custom-call | tf_op jit(solution)/shard_map/pallas_call | solution.py:222
  32.2 0.0 copy-start.13
  32.2 0.0 copy-start.12
  32.2 0.0 copy-start.10
  32.2 0.0 collective-permute-start.2
  32.2 2.9 %collective-permute-start.3 = (f32[16,144,128]{2,1,0:T(8,128)}, f32[16,144,128]{2,1,0:T(8,128)S(1)}, u32[]{:S(2)}, u32[]{:S(2)}) collective-permute-start(f32[16,144,128]{2,1,0:T(8,128)} %get-tuple-element.18), channel_id=1, source_target_pairs={{0,7},{1,0},{2,1},{3,2},{4,3},{5,4},{6,5},{7,6},{8,15},{9,8},{10,9... | collective-permute-start | bytes 3538952 | tf_op jit(solution)/shard_map/ppermute | solution.py:33
  35.2 1.2 collective-permute-start
  36.4 4.2 %collective-permute-start.1 = (f32[4,560,128]{2,1,0:T(8,128)}, f32[4,560,128]{2,1,0:T(8,128)}, u32[]{:S(2)}, u32[]{:S(2)}) collective-permute-start(f32[4,560,128]{2,1,0:T(8,128)} %get-tuple-element.16), channel_id=1, source_target_pairs={{0,120},{1,121},{2,122},{3,123},{4,124},{5,125},{6,126},{7,127},{8... | collective-permute-start | bytes 3440648 | tf_op jit(solution)/shard_map/ppermute | solution.py:33
  40.5 0.0 collective-permute-start.4
  40.5 0.0 all-to-all-done.got_any.got
  40.5 0.9 copy-done
  41.4 17.6 %shard_map.105 = (f32[2,16,16,128]{3,2,1,0:T(8,128)}, f32[16,16,128]{2,1,0:T(8,128)}) custom-call(f32[128,1,1408]{2,1,0:T(1,128)} %copy-done, f32[128,1,1408]{2,1,0:T(1,128)} %copy-done), custom_call_target="tpu_custom_call" | custom-call | tf_op jit(solution)/shard_map/pallas_call | solution.py:157
  59.0 0.8 fusion.1
  59.8 6.3 %collective-permute-done.4.c00 = f32[216,128]{1,0:T(8,128)S(1)} collective-permute-done((f32[216,128]{1,0:T(8,128)}, f32[216,128]{1,0:T(8,128)S(1)}, u32[]{:S(2)}, u32[]{:S(2)}) %collective-permute-start.4) | collective-permute-done | bytes 110624 | tf_op jit(solution)/shard_map/ppermute | solution.py:33
  66.1 0.0 collective-permute-start.8
  66.1 7.1 %collective-permute-done.8 = f32[3,16,128]{2,1,0:T(8,128)S(1)} collective-permute-done((f32[3,16,128]{2,1,0:T(8,128)S(1)}, f32[3,16,128]{2,1,0:T(8,128)S(1)}, u32[]{:S(2)}, u32[]{:S(2)}) %collective-permute-start.8) | collective-permute-done | bytes 24608 | tf_op jit(solution)/shard_map/ppermute | solution.py:33
  73.2 0.0 collective-permute-start.5
  73.3 7.7 %collective-permute-done.5.c01 = f32[216,128]{1,0:T(8,128)S(1)} collective-permute-done((f32[216,128]{1,0:T(8,128)S(1)}, f32[216,128]{1,0:T(8,128)S(1)}, u32[]{:S(2)}, u32[]{:S(2)}) %collective-permute-start.5) | collective-permute-done | bytes 110624 | tf_op jit(solution)/shard_map/ppermute | solution.py:33
  80.9 0.6 collective-permute-start.9
  81.5 0.9 constant_dynamic-update-slice_fusion.1
  82.4 2.4 %collective-permute-done.9 = f32[3,16,128]{2,1,0:T(8,128)S(1)} collective-permute-done((f32[3,16,128]{2,1,0:T(8,128)S(1)}, f32[3,16,128]{2,1,0:T(8,128)S(1)}, u32[]{:S(2)}, u32[]{:S(2)}) %collective-permute-start.9) | collective-permute-done | bytes 24608 | tf_op jit(solution)/shard_map/ppermute | solution.py:33
  84.7 0.0 copy-done.12
  84.8 1.8 %collective-permute-start.6 = (f32[216,128]{1,0:T(8,128)S(1)}, f32[216,128]{1,0:T(8,128)S(1)}, u32[]{:S(2)}, u32[]{:S(2)}) collective-permute-start(f32[216,128]{1,0:T(8,128)S(1)} %copy-done.12), channel_id=1, source_target_pairs={{0,121},{1,122},{2,123},{3,124},{4,125},{5,126},{6,127},{7,120},{8... | collective-permute-start | bytes 331784 | tf_op jit(solution)/shard_map/ppermute | solution.py:33
  86.6 5.5 %collective-permute-done.6.c10 = f32[216,128]{1,0:T(8,128)S(1)} collective-permute-done((f32[216,128]{1,0:T(8,128)S(1)}, f32[216,128]{1,0:T(8,128)S(1)}, u32[]{:S(2)}, u32[]{:S(2)}) %collective-permute-start.6) | collective-permute-done | bytes 110624 | tf_op jit(solution)/shard_map/ppermute | solution.py:33
  92.1 6.3 %collective-permute-start.7 = (f32[216,128]{1,0:T(8,128)S(1)}, f32[216,128]{1,0:T(8,128)S(1)}, u32[]{:S(2)}, u32[]{:S(2)}) collective-permute-start(f32[216,128]{1,0:T(8,128)S(1)} %copy-done.11), channel_id=1, source_target_pairs={{0,127},{1,120},{2,121},{3,122},{4,123},{5,124},{6,125},{7,126},{8... | collective-permute-start | bytes 331784 | tf_op jit(solution)/shard_map/ppermute | solution.py:33
  98.4 3.4 %collective-permute-done.7.c11 = f32[216,128]{1,0:T(8,128)S(1)} collective-permute-done((f32[216,128]{1,0:T(8,128)S(1)}, f32[216,128]{1,0:T(8,128)S(1)}, u32[]{:S(2)}, u32[]{:S(2)}) %collective-permute-start.7) | collective-permute-done | bytes 110624 | tf_op jit(solution)/shard_map/ppermute | solution.py:33
  101.8 1.3 collective-permute-start.11
  103.1 1.7 %collective-permute-done.11.attach_high = f32[22,3,128]{2,1,0:T(4,128)S(1)} collective-permute-done((f32[22,3,128]{2,1,0:T(4,128)S(1)}, f32[22,3,128]{2,1,0:T(4,128)S(1)}, u32[]{:S(2)}, u32[]{:S(2)}) %collective-permute-start.11) | collective-permute-done | bytes 33824 | tf_op jit(solution)/shard_map/ppermute | solution.py:33
  104.8 0.7 collective-permute-start.10
  105.5 4.0 %collective-permute-done.10.attach_low = f32[22,3,128]{2,1,0:T(4,128)S(1)} collective-permute-done((f32[22,3,128]{2,1,0:T(4,128)S(1)}, f32[22,3,128]{2,1,0:T(4,128)S(1)}, u32[]{:S(2)}, u32[]{:S(2)}) %collective-permute-start.10) | collective-permute-done | bytes 33824 | tf_op jit(solution)/shard_map/ppermute | solution.py:33
  109.5 0.0 collective-permute-done.wide_low
  109.5 0.0 collective-permute-done.1.wide_high
  109.5 0.0 collective-permute-done.2.side_low
  109.5 0.0 copy-start.1
  109.5 0.0 collective-permute-done.3.side_high
  109.6 0.8 broadcast_in_dim.2.rate
  110.3 0.0 copy-done.5
  110.4 0.0 copy-done.6
  110.4 0.2 copy-done.1
  110.5 0.4 copy-done.2
  111.0 25.7 %shard_map.107 = f32[32,16,16,128]{3,2,1,0:T(8,128)} custom-call(f32[16,512,128]{2,1,0:T(8,128)} %get-tuple-element.14.own, f32[4,560,128]{2,1,0:T(8,128)} %collective-permute-done.wide_low, f32[4,560,128]{2,1,0:T(8,128)} %collective-permute-done.1.wide_high, f32[16,144,128]{2,1,0:T(8,128)} %copy-done.1, f32[16,144,128]{2,1,0:T(8,128)} %copy-done.2, ...), custom_call_target="tpu_custom_call" | custom-call | tf_op jit(solution)/shard_map/pallas_call | solution.py:454
  (21 shorter events, 0.1 us)
Async XLA Ops:
  9.1 31.4 %all-to-all-start = ((f32[128,1,1408]{2,1,0:T(1,128)}), f32[128,1,1408]{2,1,0:T(1,128)S(1)}, u32[]{:S(2)}, u32[]{:S(2)}) async-start(f32[128,1,1408]{2,1,0:T(1,128)} %shard_map.104), calls=%async_computation | async-start | bytes 1441792 | tf_op jit(solution)/shard_map/all_to_all | solution.py:496
  32.2 41.1 %copy-start.13 = (f32[216,128]{1,0:T(8,128)S(1)}, f32[216,128]{1,0:T(8,128)}, u32[]{:S(2)}) copy-start(f32[216,128]{1,0:T(8,128)} %get-tuple-element.20) | copy-start | bytes 331780
  32.2 52.6 %copy-start.12 = (f32[216,128]{1,0:T(8,128)S(1)}, f32[216,128]{1,0:T(8,128)}, u32[]{:S(2)}) copy-start(f32[216,128]{1,0:T(8,128)} %get-tuple-element.21) | copy-start | bytes 331780
  32.2 59.9 %copy-start.11 = (f32[216,128]{1,0:T(8,128)S(1)}, f32[216,128]{1,0:T(8,128)}, u32[]{:S(2)}) copy-start(f32[216,128]{1,0:T(8,128)} %get-tuple-element.22) | copy-start | bytes 331780
  32.2 77.4 %copy-start.10 = (f32[32]{0:T(128)S(1)}, f32[32]{0:T(128)}, u32[]{:S(2)}) copy-start(f32[32]{0:T(128)} %param.11) | copy-start | bytes 388
  32.2 77.3 %collective-permute-start.2 = (f32[16,144,128]{2,1,0:T(8,128)}, f32[16,144,128]{2,1,0:T(8,128)S(1)}, u32[]{:S(2)}, u32[]{:S(2)}) collective-permute-start(f32[16,144,128]{2,1,0:T(8,128)} %get-tuple-element.17), channel_id=1, source_target_pairs={{0,1},{1,2},{2,3},{3,4},{4,5},{5,6},{6,7},{7,0},{8,9},{9,10},{10,1... | collective-permute-start | bytes 3538952 | tf_op jit(solution)/shard_map/ppermute | solution.py:33
  32.2 77.3 %collective-permute-start.3 = (f32[16,144,128]{2,1,0:T(8,128)}, f32[16,144,128]{2,1,0:T(8,128)S(1)}, u32[]{:S(2)}, u32[]{:S(2)}) collective-permute-start(f32[16,144,128]{2,1,0:T(8,128)} %get-tuple-element.18), channel_id=1, source_target_pairs={{0,7},{1,0},{2,1},{3,2},{4,3},{5,4},{6,5},{7,6},{8,15},{9,8},{10,9... | collective-permute-start | bytes 3538952 | tf_op jit(solution)/shard_map/ppermute | solution.py:33
  35.2 74.3 %collective-permute-start = (f32[4,560,128]{2,1,0:T(8,128)}, f32[4,560,128]{2,1,0:T(8,128)}, u32[]{:S(2)}, u32[]{:S(2)}) collective-permute-start(f32[4,560,128]{2,1,0:T(8,128)} %get-tuple-element.15), channel_id=1, source_target_pairs={{0,8},{1,9},{2,10},{3,11},{4,12},{5,13},{6,14},{7,15},{8,16},{9,17... | collective-permute-start | bytes 3440648 | tf_op jit(solution)/shard_map/ppermute | solution.py:33
  36.4 73.2 %collective-permute-start.1 = (f32[4,560,128]{2,1,0:T(8,128)}, f32[4,560,128]{2,1,0:T(8,128)}, u32[]{:S(2)}, u32[]{:S(2)}) collective-permute-start(f32[4,560,128]{2,1,0:T(8,128)} %get-tuple-element.16), channel_id=1, source_target_pairs={{0,120},{1,121},{2,122},{3,123},{4,124},{5,125},{6,126},{7,127},{8... | collective-permute-start | bytes 3440648 | tf_op jit(solution)/shard_map/ppermute | solution.py:33
  40.5 25.6 %collective-permute-start.4 = (f32[216,128]{1,0:T(8,128)}, f32[216,128]{1,0:T(8,128)S(1)}, u32[]{:S(2)}, u32[]{:S(2)}) collective-permute-start(f32[216,128]{1,0:T(8,128)} %get-tuple-element.19), channel_id=1, source_target_pairs={{0,9},{1,10},{2,11},{3,12},{4,13},{5,14},{6,15},{7,8},{8,17},{9,18... | collective-permute-start | bytes 331784 | tf_op jit(solution)/shard_map/ppermute | solution.py:33
  40.5 0.9 copy-start
  66.1 44.3 %copy-start.4 = (f32[216,128]{1,0:T(8,128)}, f32[216,128]{1,0:T(8,128)S(1)}, u32[]{:S(2)}) copy-start(f32[216,128]{1,0:T(8,128)S(1)} %collective-permute-done.4.c00) | copy-start | bytes 331780
  66.1 7.1 %collective-permute-start.8 = (f32[3,16,128]{2,1,0:T(8,128)S(1)}, f32[3,16,128]{2,1,0:T(8,128)S(1)}, u32[]{:S(2)}, u32[]{:S(2)}) collective-permute-start(f32[3,16,128]{2,1,0:T(8,128)S(1)} %get-tuple-element.27), channel_id=1, source_target_pairs={{0,8},{1,9},{2,10},{3,11},{4,12},{5,13},{6,14},{7,15},{8,16},{9,17... | collective-permute-start | bytes 73736 | tf_op jit(solution)/shard_map/ppermute | solution.py:33
  73.2 7.7 %collective-permute-start.5 = (f32[216,128]{1,0:T(8,128)S(1)}, f32[216,128]{1,0:T(8,128)S(1)}, u32[]{:S(2)}, u32[]{:S(2)}) collective-permute-start(f32[216,128]{1,0:T(8,128)S(1)} %copy-done.13), channel_id=1, source_target_pairs={{0,15},{1,8},{2,9},{3,10},{4,11},{5,12},{6,13},{7,14},{8,23},{9,16... | collective-permute-start | bytes 331784 | tf_op jit(solution)/shard_map/ppermute | solution.py:33
  80.9 29.4 %copy-start.5 = (f32[216,128]{1,0:T(8,128)}, f32[216,128]{1,0:T(8,128)S(1)}, u32[]{:S(2)}) copy-start(f32[216,128]{1,0:T(8,128)S(1)} %collective-permute-done.5.c01) | copy-start | bytes 331780
  80.9 3.8 %collective-permute-start.9 = (f32[3,16,128]{2,1,0:T(8,128)S(1)}, f32[3,16,128]{2,1,0:T(8,128)S(1)}, u32[]{:S(2)}, u32[]{:S(2)}) collective-permute-start(f32[3,16,128]{2,1,0:T(8,128)S(1)} %get-tuple-element.26), channel_id=1, source_target_pairs={{0,120},{1,121},{2,122},{3,123},{4,124},{5,125},{6,126},{7,127},{8... | collective-permute-start | bytes 73736 | tf_op jit(solution)/shard_map/ppermute | solution.py:33
  84.8 7.3 %collective-permute-start.6 = (f32[216,128]{1,0:T(8,128)S(1)}, f32[216,128]{1,0:T(8,128)S(1)}, u32[]{:S(2)}, u32[]{:S(2)}) collective-permute-start(f32[216,128]{1,0:T(8,128)S(1)} %copy-done.12), channel_id=1, source_target_pairs={{0,121},{1,122},{2,123},{3,124},{4,125},{5,126},{6,127},{7,120},{8... | collective-permute-start | bytes 331784 | tf_op jit(solution)/shard_map/ppermute | solution.py:33
  86.6 23.7 %copy-start.3 = (f32[22,16,128]{2,1,0:T(8,128)}, f32[22,16,128]{2,1,0:T(8,128)S(1)}, u32[]{:S(2)}) copy-start(f32[22,16,128]{2,1,0:T(8,128)S(1)} %constant_dynamic-update-slice_fusion.attach) | copy-start | bytes 540676
  92.1 18.3 %copy-start.6 = (f32[216,128]{1,0:T(8,128)}, f32[216,128]{1,0:T(8,128)S(1)}, u32[]{:S(2)}) copy-start(f32[216,128]{1,0:T(8,128)S(1)} %collective-permute-done.6.c10) | copy-start | bytes 331780
  92.1 9.7 %collective-permute-start.7 = (f32[216,128]{1,0:T(8,128)S(1)}, f32[216,128]{1,0:T(8,128)S(1)}, u32[]{:S(2)}, u32[]{:S(2)}) collective-permute-start(f32[216,128]{1,0:T(8,128)S(1)} %copy-done.11), channel_id=1, source_target_pairs={{0,127},{1,120},{2,121},{3,122},{4,123},{5,124},{6,125},{7,126},{8... | collective-permute-start | bytes 331784 | tf_op jit(solution)/shard_map/ppermute | solution.py:33
  101.8 8.5 %copy-start.7 = (f32[216,128]{1,0:T(8,128)}, f32[216,128]{1,0:T(8,128)S(1)}, u32[]{:S(2)}) copy-start(f32[216,128]{1,0:T(8,128)S(1)} %collective-permute-done.7.c11) | copy-start | bytes 331780
  101.8 3.0 %collective-permute-start.11 = (f32[22,3,128]{2,1,0:T(4,128)S(1)}, f32[22,3,128]{2,1,0:T(4,128)S(1)}, u32[]{:S(2)}, u32[]{:S(2)}) collective-permute-start(f32[22,3,128]{2,1,0:T(4,128)S(1)} %get-tuple-element.24), channel_id=1, source_target_pairs={{0,7},{1,0},{2,1},{3,2},{4,3},{5,4},{6,5},{7,6},{8,15},{9,8},{10,9... | collective-permute-start | bytes 101384 | tf_op jit(solution)/shard_map/ppermute | solution.py:33
  104.8 5.6 %copy-start.8 = (f32[22,3,128]{2,1,0:T(4,128)}, f32[22,3,128]{2,1,0:T(4,128)S(1)}, u32[]{:S(2)}) copy-start(f32[22,3,128]{2,1,0:T(4,128)S(1)} %collective-permute-done.11.attach_high) | copy-start | bytes 101380
  104.8 4.7 %collective-permute-start.10 = (f32[22,3,128]{2,1,0:T(4,128)S(1)}, f32[22,3,128]{2,1,0:T(4,128)S(1)}, u32[]{:S(2)}, u32[]{:S(2)}) collective-permute-start(f32[22,3,128]{2,1,0:T(4,128)S(1)} %get-tuple-element.25), channel_id=1, source_target_pairs={{0,1},{1,2},{2,3},{3,4},{4,5},{5,6},{6,7},{7,0},{8,9},{9,10},{10,1... | collective-permute-start | bytes 101384 | tf_op jit(solution)/shard_map/ppermute | solution.py:33
  109.5 0.9 copy-start.9
  109.5 1.0 copy-start.1
  109.6 1.4 %copy-start.2 = (f32[16,144,128]{2,1,0:T(8,128)}, f32[16,144,128]{2,1,0:T(8,128)S(1)}, u32[]{:S(2)}) copy-start(f32[16,144,128]{2,1,0:T(8,128)S(1)} %collective-permute-done.3.side_high) | copy-start | bytes 3538948
where the time goes:
time: 139 us; the launch traced here: 137 us
  Pallas kernels  59.1 us (43%)
  waiting for transfers between devices  38.1 us (27%)
  starting transfers between devices  30.1 us (22%)
  local copies, waits for them, and re-layouts  7.27 us (5%)
    ppermute x12, waiting for transfers between devices, rolled(): return lax.ppermute(block, AXES, pairs)  38.1 us
    pallas_call x1, Pallas kernels, transported(): pl.pallas_call(transport_kernel, out_shape=jax.ShapeDtypeStruct((32, 16,...  25.7 us
    ppermute x12, starting transfers between devices, rolled(): return lax.ppermute(block, AXES, pairs)  19 us
    pallas_call x1, Pallas kernels, deposited(): pl.pallas_call(deposit_kernel, out_shape=(jax.ShapeDtypeStruct((2, 16, 16...  17.6 us
    pallas_call x1, Pallas kernels, strips(): pl.pallas_call(strips_kernel, grid=(16,), out_shape=(rows(16, 512),) + (r...  11.9 us
    all_to_all x1, starting transfers between devices, body(): got = lax.all_to_all(sent, AXES, split_axis=0, concat_axis=0, tiled=True)  11.1 us
    unnamed x32, local copies, waits for them, and re-layouts  4.87 us
    pallas_call x1, Pallas kernels, pack(): pl.pallas_call(pack_kernel, out_shape=jax.ShapeDtypeStruct((devices, 1, 1...  3.88 us
  transfers between devices with their start and end apart: 13, of which 8 were waited for; matrix products, arithmetic and copies ran while one was open for 1% of the time, Pallas kernels for 22%

commit v1 on v0

v1 whole, which is shorter than its diff:
```python
import functools

import jax
import jax.numpy as jnp
from jax import lax
from jax.experimental import pallas as pl
from jax.experimental.pallas import tpu as pltpu
from jax.sharding import PartitionSpec as P

WIN = 4
DEPTH = 4
GROUP = 8
AXES = ("wide", "narrow")
VMEM_BYTES = 60 * 1024 * 1024

CORNER = [(a, b) for a in range(DEPTH - 1) for b in range(DEPTH - 1 - a)]


def params(**more):
    return pltpu.CompilerParams(vmem_limit_bytes=VMEM_BYTES, **more)


def rolled(block, wide_step, narrow_step):
    wide_count, narrow_count = lax.axis_size("wide"), lax.axis_size("narrow")
    pairs = [
        (
            w * narrow_count + n,
            (w + wide_step) % wide_count * narrow_count + (n + narrow_step) % narrow_count,
        )
        for w in range(wide_count)
        for n in range(narrow_count)
    ]
    return lax.ppermute(block, AXES, pairs)


def pack_kernel(
    target_of, count_of, corner_of, pos, volume, area, classes, velocity,
    sent, wide_low, wide_high, side_low, side_high,
    tally, field, speed, sem,
):
    copies = []

    def copy(source, target):
        moved = pltpu.make_async_copy(source, target, sem.at[len(copies)])
        moved.start()
        copies.append(moved)

    copy(velocity, speed)
    for k in range(32):
        copy(classes.at[k], field.at[:, :, k])

    _, clusters, bubbles = pos.shape
    devices = sent.shape[0]
    row = count_of.shape[0]
    sent[...] = jnp.zeros_like(sent)

    def clear(d, carry):
        tally[d] = 0
        return carry

    lax.fori_loop(0, devices, clear, 0, unroll=8)
    lane = lax.broadcasted_iota(jnp.int32, (1, bubbles), 1)

    def some(r, carry):
        for i in range(row):
            c = r * row + i
            target, count = target_of[0, c], count_of[i, r]
            corner_x = corner_of[0, c].astype(jnp.float32)
            corner_y = corner_of[1, c].astype(jnp.float32)
            rank = tally[target]
            tally[target] = rank + 1
            live = lane < count
            at = pl.ds(c, 1)
            rows = [
                pos[0, at, :] * 4.0,
                pos[1, at, :] * 4.0,
                pos[2, at, :] * 128.0,
                jnp.where(live, volume[at, :], 0.0),
                jnp.where(live, area[at, :], 0.0),
            ]
            for j, value in enumerate(rows):
                start = pl.multiple_of((rank * 5 + j) * bubbles, bubbles)
                sent[target, :, pl.ds(start, bubbles)] = value
            tail = sent[target, :, pl.ds(10 * bubbles, bubbles)]
            tail = jnp.where(lane == 2 * rank, corner_x, tail)
            tail = jnp.where(lane == 2 * rank + 1, corner_y, tail)
            sent[target, :, pl.ds(10 * bubbles, bubbles)] = tail
        return carry

    lax.fori_loop(0, clusters // row, some, 0)

    for moved in copies:
        moved.wait()
    arrived = len(copies)
    for out, first in ((side_low, 0), (side_high, 16 - DEPTH)):
        copy(field.at[:, pl.ds(first, DEPTH)], out.at[:, pl.ds(0, DEPTH)])
        for d in range(3):
            rows = pl.ds(8 * d, 8)
            copy(speed.at[d, :, pl.ds(first // 8 * 8, 8)], out.at[:, DEPTH, rows])
    for out, first in ((wide_low, 0), (wide_high, 16 - DEPTH)):
        copy(field.at[pl.ds(first, DEPTH)], out.at[:, pl.ds(0, 16)])
        for d in range(3):
            rows = pl.ds(16 * d % 32, 16)
            copy(speed.at[d, pl.ds(first, DEPTH)], out.at[:, 16 + 16 * d // 32, rows])
    for moved in copies[arrived:]:
        moved.wait()


def pack(target_of, count_of, corner_of, pos, volume, area, classes, velocity, devices):
    bubbles = pos.shape[2]
    smem = pl.BlockSpec(memory_space=pltpu.SMEM)
    vmem = pl.BlockSpec(memory_space=pltpu.VMEM)
    anywhere = pl.BlockSpec(memory_space=pl.ANY)
    return pl.pallas_call(
        pack_kernel,
        out_shape=(jax.ShapeDtypeStruct((devices, 1, 11 * bubbles), jnp.float32),)
        + (jax.ShapeDtypeStruct((DEPTH, WIDE_CELLS, 32, 128), jnp.float32),) * 2
        + (jax.ShapeDtypeStruct((16, SIDE_CELLS, 32, 128), jnp.float32),) * 2,
        in_specs=[smem] * 3 + [vmem] * 3 + [anywhere] * 2,
        out_specs=(vmem,) + (anywhere,) * 4,
        scratch_shapes=[
            pltpu.SMEM((devices,), jnp.int32),
            pltpu.VMEM((16, 16, 32, 128), jnp.float32),
            pltpu.VMEM((3, 16, 16, 128), jnp.float32),
            pltpu.SemaphoreType.DMA((33 + 16,)),
        ],
        compiler_params=params(),
    )(target_of, count_of, corner_of, pos, volume, area, classes, velocity)


UNROLL = 16


def halves(value):
    high = value.astype(jnp.bfloat16)
    return high, (value - high.astype(jnp.float32)).astype(jnp.bfloat16)


def across(left, right):
    return lax.dot_general(
        left, right, (((1,), (1,)), ((), ())), preferred_element_type=jnp.float32
    )


def bell(distance):
    return jnp.exp2((distance * (-0.5 * 1.4426950408889634)) * distance)


def deposit_kernel(got_any, got, deposit, attach, total, corners, sem):
    devices = got.shape[0]
    bubbles = got.shape[2] // 11
    copy = pltpu.make_async_copy(
        got_any.at[:, :, pl.ds(10 * bubbles, bubbles)], corners, sem
    )
    copy.start()
    total[...] = jnp.zeros_like(total)
    copy.wait()
    row = lax.broadcasted_iota(jnp.int32, (8, bubbles), 0)
    is_volume = row % 2 == 0
    cell_y = (row // 2).astype(jnp.float32) + 0.5
    cell_z = lax.broadcasted_iota(jnp.int32, (128, bubbles), 0).astype(jnp.float32) + 0.5

    def sources(step, carry):
        done = []
        for u in range(UNROLL):
            for slot in range(2):
                source = step * UNROLL + u
                px, py, pz, vol, are = (
                    got[source, :, (5 * slot + i) * bubbles : (5 * slot + i + 1) * bubbles]
                    for i in range(5)
                )
                share = bell(cell_y - py) * jnp.where(is_volume, vol, are)
                plane = jnp.concatenate(
                    [share * bell((i + 0.5) - px) for i in range(WIN)], axis=0
                )
                plane_high, plane_low = halves(plane)
                high, low = halves(bell(cell_z - pz))
                left = jnp.concatenate(
                    [
                        jnp.concatenate([plane_high, plane_high], axis=1),
                        jnp.concatenate([plane_low, jnp.zeros_like(plane_low)], axis=1),
                    ],
                    axis=0,
                )
                both = across(left, jnp.concatenate([high, low], axis=1))
                window = both[:32] + both[32:]
                done.append((source, slot, window))
        for source, slot, window in done:
            x = corners[source, 0, 2 * slot].astype(jnp.int32)
            y = corners[source, 0, 2 * slot + 1].astype(jnp.int32)
            for i in range(WIN):
                at = pl.ds((x + i) * 32 + y * 2, 8)
                total[at, :] = total[at, :] + window[8 * i : 8 * i + 8]
        return carry

    lax.fori_loop(0, devices // UNROLL, sources, 0)
    for x in range(16):
        gas = total[pl.ds(x * 32, 16, stride=2), :]
        face = total[pl.ds(x * 32 + 1, 16, stride=2), :]
        deposit[0, x] = gas
        deposit[1, x] = face
        attach[x] = face / (1.0 + gas)


def deposited(got):
    devices = got.shape[0]
    return pl.pallas_call(
        deposit_kernel,
        out_shape=(
            jax.ShapeDtypeStruct((2, 16, 16, 128), jnp.float32),
            jax.ShapeDtypeStruct((16, 16, 128), jnp.float32),
        ),
        in_specs=[
            pl.BlockSpec(memory_space=pl.ANY),
            pl.BlockSpec(memory_space=pltpu.VMEM),
        ],
        out_specs=(pl.BlockSpec(memory_space=pltpu.VMEM),) * 2,
        scratch_shapes=[
            pltpu.VMEM((512, 128), jnp.float32),
            pltpu.SMEM((devices, 1, 128), jnp.float32),
            pltpu.SemaphoreType.DMA,
        ],
        compiler_params=params(),
    )(got, got)


WIDE_CELLS = 16 + 2
SIDE_CELLS = DEPTH + 1
CORNER_CELLS = len(CORNER) + DEPTH - 1


def corners_kernel(side_low, side_high, low, high, held, sem):
    reach = DEPTH - 1
    count = 0

    def run(pairs):
        nonlocal count
        moved = []
        for source, target in pairs:
            moved.append(pltpu.make_async_copy(source, target, sem.at[count]))
            moved[-1].start()
            count += 1
        for one in moved:
            one.wait()

    run(
        (block.at[pl.ds(first, reach)], held.at[at, side])
        for at, block in enumerate((side_low, side_high))
        for side, first in enumerate((0, 16 - reach))
    )
    pairs = []
    for side, out in enumerate((low, high)):
        for at in range(2):
            cell = 0
            for a in range(reach):
                x, cells = reach - 1 - a if side else a, reach - a
                first = 0 if at else DEPTH - cells
                block = held.at[at, side, x]
                pairs.append((block.at[pl.ds(first, cells)], out.at[at, pl.ds(cell, cells)]))
                cell += cells
                pairs.append((block.at[DEPTH], out.at[at, len(CORNER) + a]))
    run(pairs)


def corners_of(side_low, side_high):
    anywhere = pl.BlockSpec(memory_space=pl.ANY)
    reach = DEPTH - 1
    return pl.pallas_call(
        corners_kernel,
        out_shape=(jax.ShapeDtypeStruct((2, CORNER_CELLS, 32, 128), jnp.float32),) * 2,
        in_specs=[anywhere] * 2,
        out_specs=(anywhere,) * 2,
        scratch_shapes=[
            pltpu.VMEM((2, 2, reach, SIDE_CELLS, 32, 128), jnp.float32),
            pltpu.SemaphoreType.DMA((4 + 8 * reach,)),
        ],
        compiler_params=params(),
    )(side_low, side_high)


SPAN = 16 + 2 * DEPTH
BLOCK = 2
PART = 4
ORIGIN = 8


def transport_kernel(
    classes, velocity, wide_low, wide_high, side_low, side_high, corner_low, corner_high,
    rate, attach, beside_low, beside_high, above_low, above_high,
    out,
    field, other, factor, speed, coef, load, sem, out_sem,
):
    copies = []

    def copy(source, target):
        moved = pltpu.make_async_copy(source, target, sem.at[len(copies)])
        moved.start()
        copies.append(moved)

    inner = pl.ds(DEPTH, 16)
    copy(velocity, speed.at[:, inner, pl.ds(ORIGIN, 16)])
    for block, first in ((wide_low, 0), (wide_high, 16 + DEPTH)):
        for d in range(3):
            copy(
                block.at[:, 16 + 16 * d // 32, pl.ds(16 * d % 32, 16)],
                speed.at[d, pl.ds(first, DEPTH), pl.ds(ORIGIN, 16)],
            )
    for block, first in ((side_low, 0), (side_high, ORIGIN + 16)):
        for d in range(3):
            copy(block.at[:, DEPTH, pl.ds(8 * d, 8)], speed.at[d, inner, pl.ds(first, 8)])
    turns = ((corner_low, False), (corner_high, True))
    for block, is_high in turns:
        for at, first in enumerate((0, ORIGIN + 16)):
            for a in range(DEPTH - 1):
                x = 16 + DEPTH + a if is_high else DEPTH - 1 - a
                for d in range(3):
                    copy(
                        block.at[at, len(CORNER) + a, pl.ds(8 * d, 8)],
                        speed.at[d, x, pl.ds(first, 8)],
                    )
    speeds = len(copies)
    for k in range(32):
        copy(classes.at[k], field.at[inner, inner, k])
    for block, first in ((wide_low, 0), (wide_high, 16 + DEPTH)):
        copy(block.at[:, pl.ds(0, 16)], field.at[pl.ds(first, DEPTH), inner])
    for block, first in ((side_low, 0), (side_high, 16 + DEPTH)):
        copy(block.at[:, pl.ds(0, DEPTH)], field.at[inner, pl.ds(first, DEPTH)])
    for block, is_high in turns:
        for at, first in enumerate((0, 16 + DEPTH)):
            cell = 0
            for a in range(DEPTH - 1):
                x = 16 + DEPTH + a if is_high else DEPTH - 1 - a
                run = DEPTH - 1 - a
                y = first if at else DEPTH - run
                copy(block.at[at, pl.ds(cell, run)], field.at[x, pl.ds(y, run)])
                cell += run
    for moved in copies[:speeds]:
        moved.wait()

    wide_at, narrow_at = lax.axis_index("wide"), lax.axis_index("narrow")
    wide_last, narrow_last = lax.axis_size("wide") - 1, lax.axis_size("narrow") - 1
    edges = (wide_at == 0, wide_at == wide_last, narrow_at == 0, narrow_at == narrow_last)
    spans = ((0, DEPTH), (16 + DEPTH, SPAN))

    for side, (first, last) in enumerate(spans):

        @pl.when(edges[side])
        def _(first=first, last=last):
            speed[:, first:last] = jnp.zeros((3, last - first) + speed.shape[2:], jnp.float32)

        @pl.when(edges[2 + side])
        def _(first=first, last=last):
            shift = ORIGIN - DEPTH
            speed[:, :, first + shift : last + shift] = jnp.zeros(
                (3, SPAN, last - first, 128), jnp.float32
            )

    lane = lax.broadcasted_iota(jnp.int32, (SPAN - 2, 128), 1)

    def coefficients(x, carry):
        low, high = ORIGIN - DEPTH + 1, ORIGIN + 16 + DEPTH - 1

        def at(d, dx, dy):
            return speed[d, x + dx, low + dy : high + dy, :]

        middle = [at(d, 0, 0) for d in range(3)]
        left = 0.5 * (at(0, -1, 0) + middle[0])
        right = 0.5 * (middle[0] + at(0, 1, 0))
        kept = 1.0 - jnp.maximum(right, 0.0) + jnp.minimum(left, 0.0)
        coef[1, x, low:high, :] = jnp.maximum(left, 0.0)
        coef[2, x, low:high, :] = -jnp.minimum(right, 0.0)
        left = 0.5 * (at(1, 0, -1) + middle[1])
        right = 0.5 * (middle[1] + at(1, 0, 1))
        kept = kept - jnp.maximum(right, 0.0) + jnp.minimum(left, 0.0)
        coef[3, x, low:high, :] = jnp.maximum(left, 0.0)
        coef[4, x, low:high, :] = -jnp.minimum(right, 0.0)
        before = jnp.where(lane == 0, 0.0, pltpu.roll(middle[2], 1, 1))
        after = jnp.where(lane == 127, 0.0, pltpu.roll(middle[2], 127, 1))
        left, right = 0.5 * (before + middle[2]), 0.5 * (middle[2] + after)
        kept = kept - jnp.maximum(right, 0.0) + jnp.minimum(left, 0.0)
        coef[5, x, low:high, :] = jnp.where(lane == 0, 0.0, jnp.maximum(left, 0.0))
        coef[6, x, low:high, :] = jnp.where(lane == 127, 0.0, -jnp.minimum(right, 0.0))
        coef[0, x, low:high, :] = kept
        return carry

    lax.fori_loop(1, SPAN - 1, coefficients, 0)
    for moved in copies[speeds:]:
        moved.wait()
    for side, (first, last) in enumerate(spans):

        @pl.when(edges[side])
        def _(first=first, last=last):
            field[first:last] = jnp.zeros((last - first, SPAN, 32, 128), jnp.float32)

        @pl.when(edges[2 + side])
        def _(first=first, last=last):
            field[:, first:last] = jnp.zeros((SPAN, last - first, 32, 128), jnp.float32)


    groups = 32 // GROUP
    at_class = lax.broadcasted_iota(jnp.int32, (GROUP, 128), 0)
    rates = []
    for g in range(groups):
        value = jnp.zeros((GROUP, 128), jnp.float32)
        for i in range(GROUP):
            value = jnp.where(at_class == i, -rate[g * GROUP + i], value)
        rates.append(value)
    reach = DEPTH - 1
    load[1:DEPTH, 1 : SPAN - 1, :] = above_low[...]
    load[DEPTH + 16 : SPAN - 1, 1 : SPAN - 1, :] = above_high[...]
    load[DEPTH : DEPTH + 16, 1:DEPTH, :] = beside_low[...]
    load[DEPTH : DEPTH + 16, DEPTH : DEPTH + 16, :] = attach[...]
    load[DEPTH : DEPTH + 16, DEPTH + 16 : SPAN - 1, :] = beside_high[...]

    def row_of_step(step, reach, x, source, target, live):
        def cell(dx, y, g):
            return source[x + dx, y, g * GROUP : (g + 1) * GROUP, :]

        first, last = DEPTH - reach, DEPTH + 16 + reach
        before = [cell(0, first - 1, g) for g in range(groups)]
        now = [cell(0, first, g) for g in range(groups)]
        done = []
        for y in range(first, last):
            after = [cell(0, y + 1, g) for g in range(groups)]
            yv = y + ORIGIN - DEPTH
            k = [
                jnp.broadcast_to(coef[i, x, yv : yv + 1, :], (GROUP, 128)) for i in range(7)
            ]
            if step == 0:
                kill = live
                if y < DEPTH:
                    kill = kill & ~edges[2]
                elif y >= DEPTH + 16:
                    kill = kill & ~edges[3]
                kill = kill.astype(jnp.float32)
                loaded = load[x, y : y + 1, :]
            for g in range(groups):
                value = k[0] * now[g]
                value = value + k[1] * cell(-1, y, g)
                value = value + k[2] * cell(1, y, g)
                value = value + k[3] * before[g]
                value = value + k[4] * after[g]
                value = value + k[5] * pltpu.roll(now[g], 1, 1)
                value = value + k[6] * pltpu.roll(now[g], 127, 1)
                at = (x, y, slice(g * GROUP, (g + 1) * GROUP))
                if step == 0:
                    scale = jnp.exp(rates[g] * loaded) * kill
                    done.append((factor, at, scale))
                else:
                    scale = factor[at]
                done.append((target, at, value * scale))
            before, now = now, after
            if (y - first) % BLOCK == BLOCK - 1 or y == last - 1:
                for ref, at, value in done:
                    ref[at] = value
                done = []

    source, target = field, other
    for step in range(DEPTH):
        reach = DEPTH - 1 - step

        def middle_rows(i, carry, step=step, reach=reach, source=source, target=target):
            x = DEPTH + 2 * i
            live = jnp.bool_(True)
            row_of_step(step, reach, x, source, target, live)
            row_of_step(step, reach, x + 1, source, target, live)
            return carry

        if step < DEPTH - 1:
            lax.fori_loop(0, 8, middle_rows, 0)
        else:
            for part in range(0, 16, PART):
                lax.fori_loop(part // 2, (part + PART) // 2, middle_rows, 0)
                for k in range(32):
                    pltpu.make_async_copy(
                        target.at[pl.ds(DEPTH + part, PART), inner, k],
                        out.at[k, pl.ds(part, PART)],
                        out_sem,
                    ).start()
        for away in range(1, reach + 1):

            def outer(i, carry, away=away, step=step, reach=reach, source=source, target=target):
                x = DEPTH - away + i * (15 + 2 * away)
                live = jnp.where(i == 0, wide_at != 0, wide_at != wide_last)
                row_of_step(step, reach - away, x, source, target, live)
                return carry

            lax.fori_loop(0, 2, outer, 0)
        source, target = target, source
    pltpu.make_async_copy(out, out, out_sem).wait()


def transported(classes, velocity, halos, rate, *attach):
    vmem = pl.BlockSpec(memory_space=pltpu.VMEM)
    anywhere = pl.BlockSpec(memory_space=pl.ANY)
    return pl.pallas_call(
        transport_kernel,
        out_shape=jax.ShapeDtypeStruct((32, 16, 16, 128), jnp.float32),
        in_specs=[anywhere] * 8 + [pl.BlockSpec(memory_space=pltpu.SMEM)] + [vmem] * 5,
        out_specs=anywhere,
        scratch_shapes=[
            pltpu.VMEM((SPAN, SPAN, 32, 128), jnp.float32),
            pltpu.VMEM((SPAN, SPAN, 32, 128), jnp.float32),
            pltpu.VMEM((SPAN, SPAN, 32, 128), jnp.float32),
            pltpu.VMEM((3, SPAN, 32, 128), jnp.float32),
            pltpu.VMEM((7, SPAN, 32, 128), jnp.float32),
            pltpu.VMEM((SPAN, SPAN, 128), jnp.float32),
            pltpu.SemaphoreType.DMA((97,)),
            pltpu.SemaphoreType.DMA,
        ],
        compiler_params=params(),
    )(classes, velocity, *halos, rate, *attach)


def body(
    classes,
    velocity,
    attach_rate,
    bubble_pos,
    bubble_volume,
    bubble_area,
    bubble_count,
    cluster_target,
    cluster_offset,
):
    devices = lax.axis_size("wide") * lax.axis_size("narrow")
    sent, out_low, out_high, aside_low, aside_high = pack(
        cluster_target.T,
        bubble_count.T,
        cluster_offset.T,
        jnp.transpose(bubble_pos, (1, 0, 2)),
        bubble_volume,
        bubble_area,
        classes,
        velocity,
        devices,
    )
    got = lax.all_to_all(sent, AXES, split_axis=0, concat_axis=0, tiled=True)

    side_low, side_high = rolled(aside_high, 0, 1), rolled(aside_low, 0, -1)
    turn_low, turn_high = corners_of(side_low, side_high)
    got, turn_low, turn_high, out_low, out_high = lax.optimization_barrier(
        (got, turn_low, turn_high, out_low, out_high)
    )
    wide_low, wide_high = rolled(out_high, 1, 0), rolled(out_low, -1, 0)
    corner_low, corner_high = rolled(turn_high, 1, 0), rolled(turn_low, -1, 0)
    deposit, attach = deposited(got)
    reach = DEPTH - 1
    beside_low = rolled(attach[:, -reach:], 0, 1)
    beside_high = rolled(attach[:, :reach], 0, -1)

    def across_sides(rows):
        return jnp.concatenate([beside_low[rows], attach[rows], beside_high[rows]], axis=1)

    last = across_sides(slice(-reach, None))
    first = across_sides(slice(0, reach))
    above_low, above_high = rolled(last, 1, 0), rolled(first, -1, 0)
    halos = (wide_low, wide_high, side_low, side_high, corner_low, corner_high)
    return deposit, transported(
        classes, velocity, halos, attach_rate,
        attach, beside_low, beside_high, above_low, above_high,
    )


def solution(mesh):
    return jax.shard_map(
        body,
        mesh=mesh,
        in_specs=(
            P(None, "wide", "narrow", None),
            P(None, "wide", "narrow", None),
            P(),
            P(("wide", "narrow"), None, None),
            P(("wide", "narrow"), None),
            P(("wide", "narrow"), None),
            P(("wide", "narrow"), None),
            P(("wide", "narrow"), None),
            P(("wide", "narrow"), None),
        ),
        out_specs=(P(None, "wide", "narrow", None), P(None, "wide", "narrow", None)),
        check_vma=False,
    )
```

time: 139 us -> 106 us (0.76); the launches traced: 137 us -> 105 us
  Pallas kernels: 59.1 us -> 43.5 us
  waiting for transfers between devices: 38.1 us -> 28.8 us
  starting transfers between devices: 30.1 us -> 27.3 us
  local copies, waits for them, and re-layouts: 7.27 us -> 4.93 us
    ppermute x12 -> x10, waiting for transfers between devices: 38.1 us -> 28.8 us  [rolled(): return lax.ppermute(block, AXES, pairs)]
    pallas_call x2, Pallas kernels: 15.8 us -> 9.11 us  [the longest x1 6.73 us: pack(): pl.pallas_call(pack_kernel, out_shape=(jax.ShapeDtypeStruct((devices, 1,...]
    pallas_call x1, Pallas kernels: 17.6 us -> 11.8 us  [deposited(): pl.pallas_call(deposit_kernel, out_shape=(jax.ShapeDtypeStruct((2, 16, 16...]
    pallas_call x1, Pallas kernels: 25.7 us -> 22.6 us  [transported(): pl.pallas_call(transport_kernel, out_shape=jax.ShapeDtypeStruct((32, 16,...]
    all_to_all x1, starting transfers between devices: 11.1 us -> 9.3 us  [body(): got = lax.all_to_all(sent, AXES, split_axis=0, concat_axis=0, tiled=True)]
    unnamed x32 -> x24, local copies, waits for them, and re-layouts: 4.87 us -> 3.27 us
    ppermute x12 -> x10, starting transfers between devices: 19 us -> 18 us  [rolled(): return lax.ppermute(block, AXES, pairs)]
  transfers between devices with their start and end apart: 13 -> 11, of which waited for: 8 -> 5; matrix products, arithmetic and copies ran while one was open for 1% -> 2% of each run, Pallas kernels for 22% -> 13%
where the time goes in v1:
time: 106 us; the launch traced here: 105 us
  Pallas kernels  43.5 us (41%)
  waiting for transfers between devices  28.8 us (27%)
  starting transfers between devices  27.3 us (26%)
  local copies, waits for them, and re-layouts  4.93 us (5%)
    ppermute x10, waiting for transfers between devices, rolled(): return lax.ppermute(block, AXES, pairs)  28.8 us
    pallas_call x1, Pallas kernels, transported(): pl.pallas_call(transport_kernel, out_shape=jax.ShapeDtypeStruct((32, 16,...  22.6 us
    ppermute x10, starting transfers between devices, rolled(): return lax.ppermute(block, AXES, pairs)  18 us
    pallas_call x1, Pallas kernels, deposited(): pl.pallas_call(deposit_kernel, out_shape=(jax.ShapeDtypeStruct((2, 16, 16...  11.8 us
    all_to_all x1, starting transfers between devices, body(): got = lax.all_to_all(sent, AXES, split_axis=0, concat_axis=0, tiled=True)  9.3 us
    pallas_call x1, Pallas kernels, pack(): pl.pallas_call(pack_kernel, out_shape=(jax.ShapeDtypeStruct((devices, 1,...  6.73 us
    unnamed x24, local copies, waits for them, and re-layouts  3.27 us
    pallas_call x1, Pallas kernels, corners_of(): pl.pallas_call(corners_kernel, out_shape=(jax.ShapeDtypeStruct((2, CORNER...  2.39 us
  transfers between devices with their start and end apart: 11, of which 5 were waited for; matrix products, arithmetic and copies ran while one was open for 2% of the time, Pallas kernels for 13%

profile of v1, /device:TPU:0, one launch (start us, length us, event | category | flops | bytes accessed | tf_op | source)
XLA Modules:
  0.0 105.4 jit_solution(12301338337147918355)
XLA Ops:
  0.6 6.7 %shard_map.104 = (f32[128,1,1408]{2,1,0:T(1,128)}, f32[4,18,32,128]{3,2,1,0:T(8,128)}, f32[4,18,32,128]{3,2,1,0:T(8,128)}, f32[16,5,32,128]{3,2,1,0:T(8,128)}, f32[16,5,32,128]{3,2,1,0:T(8,128)}) custom-call(s32[1,96]{1,0:T(1,128)} %bitcast.7, s32[8,12]{1,0:T(8,128)} %bitcast.5, s32[2,96]{1,0:T(2,128)} %bitcast.6, f32[3,96,128]{2,1,0:T(8,128)} %bitcast.4, ...), custom_call_target="tpu_custom_call" | custom-call | tf_op jit(solution)/shard_map/pallas_call | solution.py:114
  7.4 0.0 collective-permute-start
  7.4 3.6 %collective-permute-start.1 = (f32[16,5,32,128]{3,2,1,0:T(8,128)}, f32[16,5,32,128]{3,2,1,0:T(8,128)S(1)}, u32[]{:S(2)}, u32[]{:S(2)}) collective-permute-start(f32[16,5,32,128]{3,2,1,0:T(8,128)} %get-tuple-element.18), channel_id=1, source_target_pairs={{0,7},{1,0},{2,1},{3,2},{4,3},{5,4},{6,5},{7,6},{8,15},{9,8},{10,9... | collective-permute-start | bytes 3932168 | tf_op jit(solution)/shard_map/ppermute | solution.py:33
  11.0 9.3 %all-to-all-start = ((f32[128,1,1408]{2,1,0:T(1,128)}), f32[128,1,1408]{2,1,0:T(1,128)S(1)}, u32[]{:S(2)}, u32[]{:S(2)}) async-start(f32[128,1,1408]{2,1,0:T(1,128)} %get-tuple-element.16), calls=%async_computation | async-start | bytes 1441792 | tf_op jit(solution)/shard_map/all_to_all | solution.py:538
  20.3 10.7 %collective-permute-done.side_low = f32[16,5,32,128]{3,2,1,0:T(8,128)S(1)} collective-permute-done((f32[16,5,32,128]{3,2,1,0:T(8,128)}, f32[16,5,32,128]{3,2,1,0:T(8,128)S(1)}, u32[]{:S(2)}, u32[]{:S(2)}) %collective-permute-start) | collective-permute-done | bytes 1310752 | tf_op jit(solution)/shard_map/ppermute | solution.py:33
  31.0 0.0 copy-start.1
  31.0 3.0 %collective-permute-done.1.side_high = f32[16,5,32,128]{3,2,1,0:T(8,128)S(1)} collective-permute-done((f32[16,5,32,128]{3,2,1,0:T(8,128)}, f32[16,5,32,128]{3,2,1,0:T(8,128)S(1)}, u32[]{:S(2)}, u32[]{:S(2)}) %collective-permute-start.1) | collective-permute-done | bytes 1310752 | tf_op jit(solution)/shard_map/ppermute | solution.py:33
  34.0 0.0 copy-done.1
  34.0 0.0 copy-start.2
  34.0 1.1 %copy-done.2 = f32[16,5,32,128]{3,2,1,0:T(8,128)} copy-done((f32[16,5,32,128]{3,2,1,0:T(8,128)}, f32[16,5,32,128]{3,2,1,0:T(8,128)S(1)}, u32[]{:S(2)}) %copy-start.2) | copy-done | bytes 1310744
  35.1 2.4 %shard_map.105 = (f32[2,9,32,128]{3,2,1,0:T(8,128)}, f32[2,9,32,128]{3,2,1,0:T(8,128)}) custom-call(f32[16,5,32,128]{3,2,1,0:T(8,128)} %copy-done.1, f32[16,5,32,128]{3,2,1,0:T(8,128)} %copy-done.2), custom_call_target="tpu_custom_call" | custom-call | tf_op jit(solution)/shard_map/pallas_call | solution.py:268
  37.5 0.0 copy-start.11
  37.5 0.0 all-to-all-done.got_any.got
  37.5 0.0 copy-start
  37.5 2.4 %collective-permute-start.2 = (f32[4,18,32,128]{3,2,1,0:T(8,128)}, f32[4,18,32,128]{3,2,1,0:T(8,128)S(1)}, u32[]{:S(2)}, u32[]{:S(2)}) collective-permute-start(f32[4,18,32,128]{3,2,1,0:T(8,128)} %get-tuple-element.25), channel_id=1, source_target_pairs={{0,8},{1,9},{2,10},{3,11},{4,12},{5,13},{6,14},{7,15},{8,16},{9,17... | collective-permute-start | bytes 3538952 | tf_op jit(solution)/shard_map/ppermute | solution.py:33
  39.9 4.0 %collective-permute-start.3 = (f32[4,18,32,128]{3,2,1,0:T(8,128)}, f32[4,18,32,128]{3,2,1,0:T(8,128)S(1)}, u32[]{:S(2)}, u32[]{:S(2)}) collective-permute-start(f32[4,18,32,128]{3,2,1,0:T(8,128)} %get-tuple-element.26), channel_id=1, source_target_pairs={{0,120},{1,121},{2,122},{3,123},{4,124},{5,125},{6,126},{7,127},{8... | collective-permute-start | bytes 3538952 | tf_op jit(solution)/shard_map/ppermute | solution.py:33
  43.9 0.0 copy-done
  43.9 11.8 %shard_map.106 = (f32[2,16,16,128]{3,2,1,0:T(8,128)}, f32[16,16,128]{2,1,0:T(8,128)}) custom-call(f32[128,1,1408]{2,1,0:T(1,128)} %copy-done, f32[128,1,1408]{2,1,0:T(1,128)} %copy-done), custom_call_target="tpu_custom_call" | custom-call | tf_op jit(solution)/shard_map/pallas_call | solution.py:207
  55.7 0.9 fusion.1
  56.6 1.8 %collective-permute-start.7 = (f32[16,3,128]{2,1,0:T(4,128)S(1)}, f32[16,3,128]{2,1,0:T(4,128)S(1)}, u32[]{:S(2)}, u32[]{:S(2)}) collective-permute-start(f32[16,3,128]{2,1,0:T(4,128)S(1)} %get-tuple-element.32), channel_id=1, source_target_pairs={{0,7},{1,0},{2,1},{3,2},{4,3},{5,4},{6,5},{7,6},{8,15},{9,8},{10,9... | collective-permute-start | bytes 73736 | tf_op jit(solution)/shard_map/ppermute | solution.py:33
  58.3 0.8 fusion
  59.1 0.0 collective-permute-start.6
  59.1 0.1 collective-permute-start.4
  59.1 0.8 collective-permute-done.7.beside_high
  59.9 0.0 copy-done.11
  59.9 0.0 copy-start.7
  59.9 4.6 %collective-permute-start.5 = (f32[2,9,32,128]{3,2,1,0:T(8,128)S(1)}, f32[2,9,32,128]{3,2,1,0:T(8,128)S(1)}, u32[]{:S(2)}, u32[]{:S(2)}) collective-permute-start(f32[2,9,32,128]{3,2,1,0:T(8,128)S(1)} %copy-done.11), channel_id=1, source_target_pairs={{0,120},{1,121},{2,122},{3,123},{4,124},{5,125},{6,126},{7,127},{8... | collective-permute-start | bytes 884744 | tf_op jit(solution)/shard_map/ppermute | solution.py:33
  64.6 0.0 collective-permute-done.6.beside_low
  64.6 0.0 copy-start.8
  64.6 0.1 collective-permute-start.8
  64.7 11.9 %collective-permute-done.8.above_low = f32[3,22,128]{2,1,0:T(8,128)S(1)} collective-permute-done((f32[3,22,128]{2,1,0:T(8,128)S(1)}, f32[3,22,128]{2,1,0:T(8,128)S(1)}, u32[]{:S(2)}, u32[]{:S(2)}) %collective-permute-start.8) | collective-permute-done | bytes 33824 | tf_op jit(solution)/shard_map/ppermute | solution.py:33
  76.6 1.6 %collective-permute-start.9 = (f32[3,22,128]{2,1,0:T(8,128)S(1)}, f32[3,22,128]{2,1,0:T(8,128)S(1)}, u32[]{:S(2)}, u32[]{:S(2)}) collective-permute-start(f32[3,22,128]{2,1,0:T(8,128)S(1)} %pad_maximum_fusion.1), channel_id=1, source_target_pairs={{0,120},{1,121},{2,122},{3,123},{4,124},{5,125},{6,126},{7,127},{8... | collective-permute-start | bytes 101384 | tf_op jit(solution)/shard_map/ppermute | solution.py:33
  78.2 2.4 %collective-permute-done.9.above_high = f32[3,22,128]{2,1,0:T(8,128)S(1)} collective-permute-done((f32[3,22,128]{2,1,0:T(8,128)S(1)}, f32[3,22,128]{2,1,0:T(8,128)S(1)}, u32[]{:S(2)}, u32[]{:S(2)}) %collective-permute-start.9) | collective-permute-done | bytes 33824 | tf_op jit(solution)/shard_map/ppermute | solution.py:33
  80.6 0.0 collective-permute-done.4.corner_low
  80.6 0.0 collective-permute-done.5.corner_high
  80.6 0.0 copy-start.6
  80.6 0.0 collective-permute-done.2.wide_low
  80.6 0.0 copy-start.3
  80.6 0.0 collective-permute-done.3.wide_high
  80.6 0.0 copy-done.7
  80.6 0.0 copy-done.8
  80.6 0.0 copy-done.9
  80.6 0.5 copy-done.10
  81.2 0.1 copy-done.5
  81.3 0.1 copy-done.6
  81.4 0.4 copy-done.3
  81.8 1.0 copy-done.4
  82.8 22.6 %shard_map.107 = f32[32,16,16,128]{3,2,1,0:T(8,128)} custom-call(f32[32,16,16,128]{3,2,1,0:T(8,128)} %classes.3, f32[3,16,16,128]{3,2,1,0:T(8,128)} %velocity.3, f32[4,18,32,128]{3,2,1,0:T(8,128)} %copy-done.3, f32[4,18,32,128]{3,2,1,0:T(8,128)} %copy-done.4, f32[16,5,32,128]{3,2,1,0:T(8,128)} %copy-done.1, f32[16,5,32,128]{3,2,1,0:T(8,128)} %copy-done.2, ...), custom_call_target="tpu_custom_call" | custom-call | tf_op jit(solution)/shard_map/pallas_call | solution.py:496
  (8 shorter events, 0.0 us)
Async XLA Ops:
  7.4 23.6 %collective-permute-start = (f32[16,5,32,128]{3,2,1,0:T(8,128)}, f32[16,5,32,128]{3,2,1,0:T(8,128)S(1)}, u32[]{:S(2)}, u32[]{:S(2)}) collective-permute-start(f32[16,5,32,128]{3,2,1,0:T(8,128)} %get-tuple-element.17), channel_id=1, source_target_pairs={{0,1},{1,2},{2,3},{3,4},{4,5},{5,6},{6,7},{7,0},{8,9},{9,10},{10,1... | collective-permute-start | bytes 3932168 | tf_op jit(solution)/shard_map/ppermute | solution.py:33
  7.4 26.7 %collective-permute-start.1 = (f32[16,5,32,128]{3,2,1,0:T(8,128)}, f32[16,5,32,128]{3,2,1,0:T(8,128)S(1)}, u32[]{:S(2)}, u32[]{:S(2)}) collective-permute-start(f32[16,5,32,128]{3,2,1,0:T(8,128)} %get-tuple-element.18), channel_id=1, source_target_pairs={{0,7},{1,0},{2,1},{3,2},{4,3},{5,4},{6,5},{7,6},{8,15},{9,8},{10,9... | collective-permute-start | bytes 3932168 | tf_op jit(solution)/shard_map/ppermute | solution.py:33
  11.0 26.6 %all-to-all-start = ((f32[128,1,1408]{2,1,0:T(1,128)}), f32[128,1,1408]{2,1,0:T(1,128)S(1)}, u32[]{:S(2)}, u32[]{:S(2)}) async-start(f32[128,1,1408]{2,1,0:T(1,128)} %get-tuple-element.16), calls=%async_computation | async-start | bytes 1441792 | tf_op jit(solution)/shard_map/all_to_all | solution.py:538
  31.0 3.0 %copy-start.1 = (f32[16,5,32,128]{3,2,1,0:T(8,128)}, f32[16,5,32,128]{3,2,1,0:T(8,128)S(1)}, u32[]{:S(2)}) copy-start(f32[16,5,32,128]{3,2,1,0:T(8,128)S(1)} %collective-permute-done.side_low) | copy-start | bytes 3932164
  34.0 1.1 %copy-start.2 = (f32[16,5,32,128]{3,2,1,0:T(8,128)}, f32[16,5,32,128]{3,2,1,0:T(8,128)S(1)}, u32[]{:S(2)}) copy-start(f32[16,5,32,128]{3,2,1,0:T(8,128)S(1)} %collective-permute-done.1.side_high) | copy-start | bytes 3932164
  37.5 22.4 %copy-start.11 = (f32[2,9,32,128]{3,2,1,0:T(8,128)S(1)}, f32[2,9,32,128]{3,2,1,0:T(8,128)}, u32[]{:S(2)}) copy-start(f32[2,9,32,128]{3,2,1,0:T(8,128)} %get-tuple-element.28) | copy-start | bytes 884740
  37.5 6.3 %copy-start = (f32[128,1,1408]{2,1,0:T(1,128)}, f32[128,1,1408]{2,1,0:T(1,128)S(1)}, u32[]{:S(2)}) copy-start(f32[128,1,1408]{2,1,0:T(1,128)S(1)} %all-to-all-done.got_any.got) | copy-start | bytes 2162692
  37.5 43.0 %collective-permute-start.2 = (f32[4,18,32,128]{3,2,1,0:T(8,128)}, f32[4,18,32,128]{3,2,1,0:T(8,128)S(1)}, u32[]{:S(2)}, u32[]{:S(2)}) collective-permute-start(f32[4,18,32,128]{3,2,1,0:T(8,128)} %get-tuple-element.25), channel_id=1, source_target_pairs={{0,8},{1,9},{2,10},{3,11},{4,12},{5,13},{6,14},{7,15},{8,16},{9,17... | collective-permute-start | bytes 3538952 | tf_op jit(solution)/shard_map/ppermute | solution.py:33
  39.9 40.7 %collective-permute-start.3 = (f32[4,18,32,128]{3,2,1,0:T(8,128)}, f32[4,18,32,128]{3,2,1,0:T(8,128)S(1)}, u32[]{:S(2)}, u32[]{:S(2)}) collective-permute-start(f32[4,18,32,128]{3,2,1,0:T(8,128)} %get-tuple-element.26), channel_id=1, source_target_pairs={{0,120},{1,121},{2,122},{3,123},{4,124},{5,125},{6,126},{7,127},{8... | collective-permute-start | bytes 3538952 | tf_op jit(solution)/shard_map/ppermute | solution.py:33
  56.6 3.4 %collective-permute-start.7 = (f32[16,3,128]{2,1,0:T(4,128)S(1)}, f32[16,3,128]{2,1,0:T(4,128)S(1)}, u32[]{:S(2)}, u32[]{:S(2)}) collective-permute-start(f32[16,3,128]{2,1,0:T(4,128)S(1)} %get-tuple-element.32), channel_id=1, source_target_pairs={{0,7},{1,0},{2,1},{3,2},{4,3},{5,4},{6,5},{7,6},{8,15},{9,8},{10,9... | collective-permute-start | bytes 73736 | tf_op jit(solution)/shard_map/ppermute | solution.py:33
  59.1 5.5 %collective-permute-start.6 = (f32[16,3,128]{2,1,0:T(4,128)S(1)}, f32[16,3,128]{2,1,0:T(4,128)S(1)}, u32[]{:S(2)}, u32[]{:S(2)}) collective-permute-start(f32[16,3,128]{2,1,0:T(4,128)S(1)} %get-tuple-element.33), channel_id=1, source_target_pairs={{0,1},{1,2},{2,3},{3,4},{4,5},{5,6},{6,7},{7,0},{8,9},{9,10},{10,1... | collective-permute-start | bytes 73736 | tf_op jit(solution)/shard_map/ppermute | solution.py:33
  59.1 21.5 %collective-permute-start.4 = (f32[2,9,32,128]{3,2,1,0:T(8,128)}, f32[2,9,32,128]{3,2,1,0:T(8,128)S(1)}, u32[]{:S(2)}, u32[]{:S(2)}) collective-permute-start(f32[2,9,32,128]{3,2,1,0:T(8,128)} %get-tuple-element.27), channel_id=1, source_target_pairs={{0,8},{1,9},{2,10},{3,11},{4,12},{5,13},{6,14},{7,15},{8,16},{9,17... | collective-permute-start | bytes 884744 | tf_op jit(solution)/shard_map/ppermute | solution.py:33
  59.9 20.7 %copy-start.7 = (f32[16,3,128]{2,1,0:T(4,128)}, f32[16,3,128]{2,1,0:T(4,128)S(1)}, u32[]{:S(2)}) copy-start(f32[16,3,128]{2,1,0:T(4,128)S(1)} %collective-permute-done.7.beside_high) | copy-start | bytes 73732
  59.9 20.7 %collective-permute-start.5 = (f32[2,9,32,128]{3,2,1,0:T(8,128)S(1)}, f32[2,9,32,128]{3,2,1,0:T(8,128)S(1)}, u32[]{:S(2)}, u32[]{:S(2)}) collective-permute-start(f32[2,9,32,128]{3,2,1,0:T(8,128)S(1)} %copy-done.11), channel_id=1, source_target_pairs={{0,120},{1,121},{2,122},{3,123},{4,124},{5,125},{6,126},{7,127},{8... | collective-permute-start | bytes 884744 | tf_op jit(solution)/shard_map/ppermute | solution.py:33
  64.6 16.1 %copy-start.8 = (f32[16,3,128]{2,1,0:T(4,128)}, f32[16,3,128]{2,1,0:T(4,128)S(1)}, u32[]{:S(2)}) copy-start(f32[16,3,128]{2,1,0:T(4,128)S(1)} %collective-permute-done.6.beside_low) | copy-start | bytes 73732
  64.6 12.0 %collective-permute-start.8 = (f32[3,22,128]{2,1,0:T(8,128)S(1)}, f32[3,22,128]{2,1,0:T(8,128)S(1)}, u32[]{:S(2)}, u32[]{:S(2)}) collective-permute-start(f32[3,22,128]{2,1,0:T(8,128)S(1)} %pad_maximum_fusion), channel_id=1, source_target_pairs={{0,8},{1,9},{2,10},{3,11},{4,12},{5,13},{6,14},{7,15},{8,16},{9,17... | collective-permute-start | bytes 101384 | tf_op jit(solution)/shard_map/ppermute | solution.py:33
  76.6 4.0 %copy-start.9 = (f32[3,22,128]{2,1,0:T(8,128)}, f32[3,22,128]{2,1,0:T(8,128)S(1)}, u32[]{:S(2)}) copy-start(f32[3,22,128]{2,1,0:T(8,128)S(1)} %collective-permute-done.8.above_low) | copy-start | bytes 101380
  76.6 4.0 %collective-permute-start.9 = (f32[3,22,128]{2,1,0:T(8,128)S(1)}, f32[3,22,128]{2,1,0:T(8,128)S(1)}, u32[]{:S(2)}, u32[]{:S(2)}) collective-permute-start(f32[3,22,128]{2,1,0:T(8,128)S(1)} %pad_maximum_fusion.1), channel_id=1, source_target_pairs={{0,120},{1,121},{2,122},{3,123},{4,124},{5,125},{6,126},{7,127},{8... | collective-permute-start | bytes 101384 | tf_op jit(solution)/shard_map/ppermute | solution.py:33
  80.6 0.6 copy-start.10
  80.6 0.7 copy-start.5
  80.6 0.8 copy-start.6
  80.6 1.2 %copy-start.3 = (f32[4,18,32,128]{3,2,1,0:T(8,128)}, f32[4,18,32,128]{3,2,1,0:T(8,128)S(1)}, u32[]{:S(2)}) copy-start(f32[4,18,32,128]{3,2,1,0:T(8,128)S(1)} %collective-permute-done.2.wide_low) | copy-start | bytes 3538948
  81.8 1.0 copy-start.4

commit v2 on v1

v2 whole, which is shorter than its diff:
```python
import functools

import jax
import jax.numpy as jnp
from jax import lax
from jax.experimental import pallas as pl
from jax.experimental.pallas import tpu as pltpu
from jax.sharding import PartitionSpec as P

WIN = 4
DEPTH = 4
REACH = DEPTH - 1
GROUP = 8
AXES = ("wide", "narrow")
VMEM_BYTES = 60 * 1024 * 1024

CORNER = [(a, b) for a in range(REACH - 1) for b in range(REACH - 1 - a)]


def params(**more):
    return pltpu.CompilerParams(vmem_limit_bytes=VMEM_BYTES, **more)


def rolled(block, wide_step, narrow_step):
    wide_count, narrow_count = lax.axis_size("wide"), lax.axis_size("narrow")
    pairs = [
        (
            w * narrow_count + n,
            (w + wide_step) % wide_count * narrow_count + (n + narrow_step) % narrow_count,
        )
        for w in range(wide_count)
        for n in range(narrow_count)
    ]
    return lax.ppermute(block, AXES, pairs)


def wide_speed(i, d):
    return 16 + 2 * i + d // 2, pl.ds(16 * (d % 2), 16)


def edges_kernel(
    classes, velocity, wide_low, wide_high, side_low, side_high, field, speed, sem
):
    copies = []

    def copy(source, target):
        moved = pltpu.make_async_copy(source, target, sem.at[len(copies)])
        moved.start()
        copies.append(moved)

    copy(velocity, speed)
    for x, row in ((0, 0), (15, 1)):
        for k in range(32):
            copy(classes.at[k, x], field.at[row, :, k])
    aside = len(copies)
    for first in (0, 1):
        for k in range(32):
            copy(classes.at[k, :, pl.ds(8 * first, 8)], field.at[pl.ds(2, 16), pl.ds(8 * first, 8), k])
    for moved in copies[:aside]:
        moved.wait()
    leaving = len(copies)
    for out, row, first in ((wide_low, 0, 0), (wide_high, 1, 16 - REACH)):
        copy(field.at[row], out.at[pl.ds(0, 16)])
        for i in range(REACH):
            for d in range(3):
                copy(speed.at[d, first + i], out.at[wide_speed(i, d)])
    for out, y in ((side_low, 0), (side_high, 15)):
        for d in range(3):
            copy(speed.at[d, :, pl.ds(y // 8 * 8, 8)], out.at[:, 1, pl.ds(8 * d, 8)])
    for moved in copies[aside:leaving]:
        moved.wait()
    for out, y in ((side_low, 0), (side_high, 15)):
        copy(field.at[pl.ds(2, 16), y], out.at[:, 0])
    for moved in copies[leaving:]:
        moved.wait()


def edges_of(classes, velocity):
    anywhere = pl.BlockSpec(memory_space=pl.ANY)
    return pl.pallas_call(
        edges_kernel,
        out_shape=(jax.ShapeDtypeStruct((16 + 2 * REACH, 32, 128), jnp.float32),) * 2
        + (jax.ShapeDtypeStruct((16, 2, 32, 128), jnp.float32),) * 2,
        in_specs=[anywhere] * 2,
        out_specs=(anywhere,) * 4,
        scratch_shapes=[
            pltpu.VMEM((18, 16, 32, 128), jnp.float32),
            pltpu.VMEM((3, 16, 16, 128), jnp.float32),
            pltpu.SemaphoreType.DMA((129 + 8 + 2 + 6 * REACH,)),
        ],
        compiler_params=params(),
    )(classes, velocity)


def pack_kernel(target_of, count_of, corner_of, pos, volume, area, sent, tally):
    _, clusters, bubbles = pos.shape
    devices = sent.shape[0]
    row = count_of.shape[0]
    sent[...] = jnp.zeros_like(sent)

    def clear(d, carry):
        tally[d] = 0
        return carry

    lax.fori_loop(0, devices, clear, 0, unroll=8)
    lane = lax.broadcasted_iota(jnp.int32, (1, bubbles), 1)

    def some(r, carry):
        for i in range(row):
            c = r * row + i
            target, count = target_of[0, c], count_of[i, r]
            corner_x = corner_of[0, c].astype(jnp.float32)
            corner_y = corner_of[1, c].astype(jnp.float32)
            rank = tally[target]
            tally[target] = rank + 1
            live = lane < count
            at = pl.ds(c, 1)
            rows = [
                pos[0, at, :] * 4.0,
                pos[1, at, :] * 4.0,
                pos[2, at, :] * 128.0,
                jnp.where(live, volume[at, :], 0.0),
                jnp.where(live, area[at, :], 0.0),
            ]
            for j, value in enumerate(rows):
                start = pl.multiple_of((rank * 5 + j) * bubbles, bubbles)
                sent[target, :, pl.ds(start, bubbles)] = value
            tail = sent[target, :, pl.ds(10 * bubbles, bubbles)]
            tail = jnp.where(lane == 2 * rank, corner_x, tail)
            tail = jnp.where(lane == 2 * rank + 1, corner_y, tail)
            sent[target, :, pl.ds(10 * bubbles, bubbles)] = tail
        return carry

    lax.fori_loop(0, clusters // row, some, 0)


def pack(target_of, count_of, corner_of, pos, volume, area, devices):
    bubbles = pos.shape[2]
    return pl.pallas_call(
        pack_kernel,
        out_shape=jax.ShapeDtypeStruct((devices, 1, 11 * bubbles), jnp.float32),
        in_specs=[pl.BlockSpec(memory_space=pltpu.SMEM)] * 3
        + [pl.BlockSpec(memory_space=pltpu.VMEM)] * 3,
        out_specs=pl.BlockSpec(memory_space=pltpu.VMEM),
        scratch_shapes=[pltpu.SMEM((devices,), jnp.int32)],
        compiler_params=params(),
    )(target_of, count_of, corner_of, pos, volume, area)


UNROLL = 32


def halves(value):
    high = value.astype(jnp.bfloat16)
    return high, (value - high.astype(jnp.float32)).astype(jnp.bfloat16)


def across(left, right):
    return lax.dot_general(
        left, right, (((1,), (1,)), ((), ())), preferred_element_type=jnp.float32
    )


def bell(distance):
    return jnp.exp2((distance * (-0.5 * 1.4426950408889634)) * distance)


def deposit_kernel(got_any, got, deposit, attach, total, corners, sem):
    devices = got.shape[0]
    bubbles = got.shape[2] // 11
    copy = pltpu.make_async_copy(
        got_any.at[:, :, pl.ds(10 * bubbles, bubbles)], corners, sem
    )
    copy.start()
    total[...] = jnp.zeros_like(total)
    copy.wait()
    row = lax.broadcasted_iota(jnp.int32, (8, bubbles), 0)
    is_volume = row % 2 == 0
    cell_y = (row // 2).astype(jnp.float32) + 0.5
    cell_z = lax.broadcasted_iota(jnp.int32, (128, bubbles), 0).astype(jnp.float32) + 0.5

    def sources(step, carry):
        done = []
        for u in range(UNROLL):
            for slot in range(2):
                source = step * UNROLL + u
                px, py, pz, vol, are = (
                    got[source, :, (5 * slot + i) * bubbles : (5 * slot + i + 1) * bubbles]
                    for i in range(5)
                )
                share = bell(cell_y - py) * jnp.where(is_volume, vol, are)
                plane = jnp.concatenate(
                    [share * bell((i + 0.5) - px) for i in range(WIN)], axis=0
                )
                plane_high, plane_low = halves(plane)
                high, low = halves(bell(cell_z - pz))
                left = jnp.concatenate(
                    [
                        jnp.concatenate([plane_high, plane_high], axis=1),
                        jnp.concatenate([plane_low, jnp.zeros_like(plane_low)], axis=1),
                    ],
                    axis=0,
                )
                both = across(left, jnp.concatenate([high, low], axis=1))
                window = both[:32] + both[32:]
                done.append((source, slot, window))
        for source, slot, window in done:
            x = corners[source, 0, 2 * slot].astype(jnp.int32)
            y = corners[source, 0, 2 * slot + 1].astype(jnp.int32)
            for i in range(WIN):
                at = pl.ds((x + i) * 32 + y * 2, 8)
                total[at, :] = total[at, :] + window[8 * i : 8 * i + 8]
        return carry

    lax.fori_loop(0, devices // UNROLL, sources, 0)
    for x in range(16):
        gas = total[pl.ds(x * 32, 16, stride=2), :]
        face = total[pl.ds(x * 32 + 1, 16, stride=2), :]
        deposit[0, x] = gas
        deposit[1, x] = face
        attach[x] = face / (1.0 + gas)


def deposited(got):
    devices = got.shape[0]
    return pl.pallas_call(
        deposit_kernel,
        out_shape=(
            jax.ShapeDtypeStruct((2, 16, 16, 128), jnp.float32),
            jax.ShapeDtypeStruct((16, 16, 128), jnp.float32),
        ),
        in_specs=[
            pl.BlockSpec(memory_space=pl.ANY),
            pl.BlockSpec(memory_space=pltpu.VMEM),
        ],
        out_specs=(pl.BlockSpec(memory_space=pltpu.VMEM),) * 2,
        scratch_shapes=[
            pltpu.VMEM((512, 128), jnp.float32),
            pltpu.SMEM((devices, 1, 128), jnp.float32),
            pltpu.SemaphoreType.DMA,
        ],
        compiler_params=params(),
    )(got, got)


SPAN = 16 + 2 * DEPTH
ORIGIN = 8
BLOCK = 2
PART = 4
GROUPS = 32 // GROUP


def fill_coefficients(speed, coef, x, low, high):
    lane = lax.broadcasted_iota(jnp.int32, (high - low, 128), 1)

    def at(d, dx, dy):
        return speed[d, x + dx, low + dy : high + dy, :]

    middle = [at(d, 0, 0) for d in range(3)]
    left = 0.5 * (at(0, -1, 0) + middle[0])
    right = 0.5 * (middle[0] + at(0, 1, 0))
    kept = 1.0 - jnp.maximum(right, 0.0) + jnp.minimum(left, 0.0)
    coef[1, x, low:high, :] = jnp.maximum(left, 0.0)
    coef[2, x, low:high, :] = -jnp.minimum(right, 0.0)
    left = 0.5 * (at(1, 0, -1) + middle[1])
    right = 0.5 * (middle[1] + at(1, 0, 1))
    kept = kept - jnp.maximum(right, 0.0) + jnp.minimum(left, 0.0)
    coef[3, x, low:high, :] = jnp.maximum(left, 0.0)
    coef[4, x, low:high, :] = -jnp.minimum(right, 0.0)
    before = jnp.where(lane == 0, 0.0, pltpu.roll(middle[2], 1, 1))
    after = jnp.where(lane == 127, 0.0, pltpu.roll(middle[2], 127, 1))
    left, right = 0.5 * (before + middle[2]), 0.5 * (middle[2] + after)
    kept = kept - jnp.maximum(right, 0.0) + jnp.minimum(left, 0.0)
    coef[5, x, low:high, :] = jnp.where(lane == 0, 0.0, jnp.maximum(left, 0.0))
    coef[6, x, low:high, :] = jnp.where(lane == 127, 0.0, -jnp.minimum(right, 0.0))
    coef[0, x, low:high, :] = kept


def move_row(source, coef, x, first, last, to_speed, finish):
    def cell(dx, y, g):
        return source[x + dx, y, g * GROUP : (g + 1) * GROUP, :]

    before = [cell(0, first - 1, g) for g in range(GROUPS)]
    now = [cell(0, first, g) for g in range(GROUPS)]
    done = []
    for y in range(first, last):
        after = [cell(0, y + 1, g) for g in range(GROUPS)]
        yv = y + to_speed
        k = [jnp.broadcast_to(coef[i, x, yv : yv + 1, :], (GROUP, 128)) for i in range(7)]
        for g in range(GROUPS):
            value = k[0] * now[g]
            value = value + k[1] * cell(-1, y, g)
            value = value + k[2] * cell(1, y, g)
            value = value + k[3] * before[g]
            value = value + k[4] * after[g]
            value = value + k[5] * pltpu.roll(now[g], 1, 1)
            value = value + k[6] * pltpu.roll(now[g], 127, 1)
            done.append(finish((x, y, slice(g * GROUP, (g + 1) * GROUP)), value))
        before, now = now, after
        if (y - first) % BLOCK == BLOCK - 1 or y == last - 1:
            for ref, at, value in done:
                ref[at] = value
            done = []


def brick_edges():
    wide_at, narrow_at = lax.axis_index("wide"), lax.axis_index("narrow")
    wide_last, narrow_last = lax.axis_size("wide") - 1, lax.axis_size("narrow") - 1
    return wide_at == 0, wide_at == wide_last, narrow_at == 0, narrow_at == narrow_last


def first_kernel(
    classes, velocity, wide_low, wide_high, side_low, side_high,
    own, out_low, out_high, aside_low, aside_high,
    field, moved, speed, coef, sem,
):
    copies = []

    def copy(source, target):
        one = pltpu.make_async_copy(source, target, sem.at[len(copies)])
        one.start()
        copies.append(one)

    inner = pl.ds(1, 16)
    copy(velocity, speed.at[:, inner, pl.ds(ORIGIN, 16)])
    for d in range(3):
        copy(wide_low.at[wide_speed(REACH - 1, d)], speed.at[d, 0, pl.ds(ORIGIN, 16)])
        copy(wide_high.at[wide_speed(0, d)], speed.at[d, 17, pl.ds(ORIGIN, 16)])
        copy(side_low.at[:, 1, pl.ds(8 * d, 8)], speed.at[d, inner, pl.ds(0, 8)])
        copy(side_high.at[:, 1, pl.ds(8 * d, 8)], speed.at[d, inner, pl.ds(ORIGIN + 16, 8)])
    speeds = len(copies)
    for k in range(32):
        copy(classes.at[k], field.at[inner, inner, k])
    copy(wide_low.at[pl.ds(0, 16)], field.at[0, inner])
    copy(wide_high.at[pl.ds(0, 16)], field.at[17, inner])
    copy(side_low.at[:, 0], field.at[inner, 0])
    copy(side_high.at[:, 0], field.at[inner, 17])
    for one in copies[:speeds]:
        one.wait()
    edges = brick_edges()
    row = jnp.zeros((18, 32, 128), jnp.float32)
    for at, x in ((0, 0), (1, 17)):

        @pl.when(edges[at])
        def _(x=x):
            for d in range(3):
                speed[d, x] = jnp.zeros((32, 128), jnp.float32)

    for at, y in ((2, 0), (3, ORIGIN + 16)):

        @pl.when(edges[at])
        def _(y=y):
            speed[:, :, y : y + 8] = jnp.zeros((3, 18, 8, 128), jnp.float32)

    def coefficients(x, carry):
        fill_coefficients(speed, coef, x, ORIGIN, ORIGIN + 16)
        return carry

    lax.fori_loop(1, 17, coefficients, 0)
    for one in copies[speeds:]:
        one.wait()
    for at, here in ((0, 0), (1, 17)):

        @pl.when(edges[at])
        def _(here=here):
            field[here] = row

        @pl.when(edges[2 + at])
        def _(here=here):
            field[:, here] = row

    def rows(i, carry):
        for x in (1 + 2 * i, 2 + 2 * i):

            def finish(at, value):
                return moved, (at[0] - 1, at[1] - 1, at[2]), value

            move_row(field, coef, x, 1, 17, ORIGIN - 1, finish)
        return carry

    lax.fori_loop(0, 8, rows, 0)
    started = len(copies)
    copy(moved.at[pl.ds(0, REACH)], out_low)
    copy(moved.at[pl.ds(16 - REACH, REACH)], out_high)
    copy(moved.at[:, pl.ds(0, REACH)], aside_low)
    copy(moved.at[:, pl.ds(16 - REACH, REACH)], aside_high)
    copy(moved, own)
    for one in copies[started:]:
        one.wait()


def first_moved(classes, velocity, *halos):
    anywhere = pl.BlockSpec(memory_space=pl.ANY)
    return pl.pallas_call(
        first_kernel,
        out_shape=(jax.ShapeDtypeStruct((16, 16, 32, 128), jnp.float32),)
        + (jax.ShapeDtypeStruct((REACH, 16, 32, 128), jnp.float32),) * 2
        + (jax.ShapeDtypeStruct((16, REACH, 32, 128), jnp.float32),) * 2,
        in_specs=[anywhere] * 6,
        out_specs=(anywhere,) * 5,
        scratch_shapes=[
            pltpu.VMEM((18, 18, 32, 128), jnp.float32),
            pltpu.VMEM((16, 16, 32, 128), jnp.float32),
            pltpu.VMEM((3, 18, 32, 128), jnp.float32),
            pltpu.VMEM((7, 18, 32, 128), jnp.float32),
            pltpu.SemaphoreType.DMA((13 + 36 + 5,)),
        ],
        compiler_params=params(),
    )(classes, velocity, *halos)


TURN = len(CORNER) + REACH - 1
TURN_CELLS = 2 * TURN + REACH


def turns_kernel(
    aside_low, aside_high, side_low, side_high, attach, beside_low, beside_high, low, high, sem
):
    copies = []
    for side, out in enumerate((low, high)):
        for at, (block, speeds) in enumerate(((aside_low, side_low), (aside_high, side_high))):
            cell = TURN * at
            for a in range(REACH - 1):
                x, cells = 15 - a if side else a, REACH - 1 - a
                first = 0 if at else REACH - cells
                copies.append((block.at[x, pl.ds(first, cells)], out.at[pl.ds(cell, cells)]))
                cell += cells
                copies.append((speeds.at[x, 1], out.at[TURN * at + len(CORNER) + a]))
    moved = [
        pltpu.make_async_copy(source, target, sem.at[i])
        for i, (source, target) in enumerate(copies)
    ]
    for one in moved:
        one.start()
    for first, out in ((0, low), (16 - REACH, high)):
        for i in range(REACH):
            out[2 * TURN + i, 0:REACH, :] = beside_low[first + i]
            out[2 * TURN + i, REACH : REACH + 16, :] = attach[first + i]
            out[2 * TURN + i, REACH + 16 : 2 * REACH + 16, :] = beside_high[first + i]
    for one in moved:
        one.wait()


def turns(*operands):
    anywhere = pl.BlockSpec(memory_space=pl.ANY)
    vmem = pl.BlockSpec(memory_space=pltpu.VMEM)
    return pl.pallas_call(
        turns_kernel,
        out_shape=(jax.ShapeDtypeStruct((TURN_CELLS, 32, 128), jnp.float32),) * 2,
        in_specs=[anywhere] * 4 + [vmem] * 3,
        out_specs=(vmem,) * 2,
        scratch_shapes=[pltpu.SemaphoreType.DMA((8 * (REACH - 1),))],
        compiler_params=params(),
    )(*operands)


def transport_kernel(
    own, velocity, out_low, out_high, aside_low, aside_high,
    wide_low, wide_high, side_low, side_high, turn_low, turn_high,
    rate, attach, beside_low, beside_high,
    out,
    field, other, factor, speed, coef, load, above, sem, out_sem,
):
    copies = []

    def copy(source, target):
        moved = pltpu.make_async_copy(source, target, sem.at[len(copies)])
        moved.start()
        copies.append(moved)

    inner = pl.ds(DEPTH, 16)
    copy(velocity, speed.at[:, inner, pl.ds(ORIGIN, 16)])
    for block, first in ((wide_low, DEPTH - REACH), (wide_high, 16 + DEPTH)):
        for i in range(REACH):
            for d in range(3):
                copy(
                    block.at[wide_speed(i, d)],
                    speed.at[d, first + i, pl.ds(ORIGIN, 16)],
                )
    for block, first in ((side_low, 0), (side_high, ORIGIN + 16)):
        for d in range(3):
            copy(block.at[:, 1, pl.ds(8 * d, 8)], speed.at[d, inner, pl.ds(first, 8)])
    for side, block in enumerate((turn_low, turn_high)):
        copy(block.at[pl.ds(2 * TURN, REACH)], above.at[side])
        for at, first in enumerate((0, ORIGIN + 16)):
            for a in range(REACH - 1):
                x = 16 + DEPTH + a if side else DEPTH - 1 - a
                for d in range(3):
                    copy(
                        block.at[TURN * at + len(CORNER) + a, pl.ds(8 * d, 8)],
                        speed.at[d, x, pl.ds(first, 8)],
                    )
    speeds = len(copies)
    copy(own, field.at[inner, inner])
    for block, first in ((out_low, DEPTH - REACH), (out_high, 16 + DEPTH)):
        copy(block, field.at[pl.ds(first, REACH), inner])
    for block, first in ((aside_low, DEPTH - REACH), (aside_high, 16 + DEPTH)):
        copy(block, field.at[inner, pl.ds(first, REACH)])
    for side, block in enumerate((turn_low, turn_high)):
        for at in range(2):
            cell = TURN * at
            for a in range(REACH - 1):
                x = 16 + DEPTH + a if side else DEPTH - 1 - a
                run = REACH - 1 - a
                y = 16 + DEPTH if at else DEPTH - run
                copy(block.at[pl.ds(cell, run)], field.at[x, pl.ds(y, run)])
                cell += run
    for moved in copies[:speeds]:
        moved.wait()

    edges = brick_edges()
    for side, (first, last) in enumerate(((0, DEPTH), (16 + DEPTH, SPAN))):

        @pl.when(edges[side])
        def _(first=first, last=last):
            speed[:, first:last] = jnp.zeros((3, last - first, 32, 128), jnp.float32)

        @pl.when(edges[2 + side])
        def _(first=first, last=last):
            shift = ORIGIN - DEPTH
            speed[:, :, first + shift : last + shift] = jnp.zeros(
                (3, SPAN, last - first, 128), jnp.float32
            )

    def coefficients(x, carry):
        fill_coefficients(speed, coef, x, ORIGIN - REACH + 1, ORIGIN + 16 + REACH - 1)
        return carry

    lax.fori_loop(DEPTH - REACH + 1, DEPTH + 16 + REACH - 1, coefficients, 0)

    at_class = lax.broadcasted_iota(jnp.int32, (GROUP, 128), 0)
    rates = []
    for g in range(GROUPS):
        value = jnp.zeros((GROUP, 128), jnp.float32)
        for i in range(GROUP):
            value = jnp.where(at_class == i, -rate[g * GROUP + i], value)
        rates.append(value)
    low, high = DEPTH - REACH, DEPTH + 16 + REACH
    load[low:DEPTH, low:high, :] = above[0, :, 0 : high - low, :]
    load[DEPTH + 16 : high, low:high, :] = above[1, :, 0 : high - low, :]
    load[DEPTH : DEPTH + 16, low:DEPTH, :] = beside_low[...]
    load[DEPTH : DEPTH + 16, DEPTH : DEPTH + 16, :] = attach[...]
    load[DEPTH : DEPTH + 16, DEPTH + 16 : high, :] = beside_high[...]
    for moved in copies[speeds:]:
        moved.wait()

    def scale_row(reach, x, source, target, live):
        for y in range(DEPTH - reach, DEPTH + 16 + reach):
            kill = live
            if y < DEPTH:
                kill = kill & ~edges[2]
            elif y >= DEPTH + 16:
                kill = kill & ~edges[3]
            kill = kill.astype(jnp.float32)
            loaded = load[x, y : y + 1, :]
            for g in range(GROUPS):
                at = (x, y, slice(g * GROUP, (g + 1) * GROUP))
                scale = jnp.exp(rates[g] * loaded) * kill
                factor[at] = scale
                target[at] = source[at] * scale

    def step_row(step, reach, x, source, target, live):
        if step == 0:
            scale_row(reach, x, source, target, live)
            return

        def finish(at, value):
            return target, at, value * factor[at]

        first, last = DEPTH - reach, DEPTH + 16 + reach
        move_row(source, coef, x, first, last, ORIGIN - DEPTH, finish)

    source, target = field, other
    for step in range(DEPTH):
        reach = REACH - step

        def middle_rows(i, carry, step=step, reach=reach, source=source, target=target):
            for x in (DEPTH + 2 * i, DEPTH + 2 * i + 1):
                step_row(step, reach, x, source, target, jnp.bool_(True))
            return carry

        if step < DEPTH - 1:
            lax.fori_loop(0, 8, middle_rows, 0)
        else:
            for part in range(0, 16, PART):
                lax.fori_loop(part // 2, (part + PART) // 2, middle_rows, 0)
                for k in range(32):
                    pltpu.make_async_copy(
                        target.at[pl.ds(DEPTH + part, PART), inner, k],
                        out.at[k, pl.ds(part, PART)],
                        out_sem,
                    ).start()
        for away in range(1, reach + 1):

            def outer(i, carry, away=away, step=step, reach=reach, source=source, target=target):
                x = DEPTH - away + i * (15 + 2 * away)
                live = ~jnp.where(i == 0, edges[0], edges[1])
                step_row(step, reach - away, x, source, target, live)
                return carry

            lax.fori_loop(0, 2, outer, 0)
        source, target = target, source
    pltpu.make_async_copy(out, out, out_sem).wait()


def transported(*operands):
    vmem = pl.BlockSpec(memory_space=pltpu.VMEM)
    anywhere = pl.BlockSpec(memory_space=pl.ANY)
    return pl.pallas_call(
        transport_kernel,
        out_shape=jax.ShapeDtypeStruct((32, 16, 16, 128), jnp.float32),
        in_specs=[anywhere] * 12 + [pl.BlockSpec(memory_space=pltpu.SMEM)] + [vmem] * 3,
        out_specs=anywhere,
        scratch_shapes=[
            pltpu.VMEM((SPAN, SPAN, 32, 128), jnp.float32),
            pltpu.VMEM((SPAN, SPAN, 32, 128), jnp.float32),
            pltpu.VMEM((SPAN, SPAN, 32, 128), jnp.float32),
            pltpu.VMEM((3, SPAN, 32, 128), jnp.float32),
            pltpu.VMEM((7, SPAN, 32, 128), jnp.float32),
            pltpu.VMEM((SPAN, SPAN, 128), jnp.float32),
            pltpu.VMEM((2, REACH, 32, 128), jnp.float32),
            pltpu.SemaphoreType.DMA((1 + 6 * REACH + 6 + 2 + 12 * (REACH - 1) + 5 + 4 * (REACH - 1),)),
            pltpu.SemaphoreType.DMA,
        ],
        compiler_params=params(),
    )(*operands)


def body(
    classes,
    velocity,
    attach_rate,
    bubble_pos,
    bubble_volume,
    bubble_area,
    bubble_count,
    cluster_target,
    cluster_offset,
):
    devices = lax.axis_size("wide") * lax.axis_size("narrow")
    edge = edges_of(classes, velocity)
    *edge, bubble_volume = lax.optimization_barrier((*edge, bubble_volume))
    sent = pack(
        cluster_target.T,
        bubble_count.T,
        cluster_offset.T,
        jnp.transpose(bubble_pos, (1, 0, 2)),
        bubble_volume,
        bubble_area,
        devices,
    )
    side_low, side_high = rolled(edge[3], 0, 1), rolled(edge[2], 0, -1)
    wide_low, wide_high = rolled(edge[1], 1, 0), rolled(edge[0], -1, 0)
    sent, side_low, side_high, wide_low, wide_high = lax.optimization_barrier(
        (sent, side_low, side_high, wide_low, wide_high)
    )
    got = lax.all_to_all(sent, AXES, split_axis=0, concat_axis=0, tiled=True)
    own, *edge = first_moved(classes, velocity, wide_low, wide_high, side_low, side_high)
    got, own, *edge = lax.optimization_barrier((got, own, *edge))
    aside_low, aside_high = rolled(edge[3], 0, 1), rolled(edge[2], 0, -1)
    out_low, out_high = rolled(edge[1], 1, 0), rolled(edge[0], -1, 0)

    deposit, attach = deposited(got)
    attach, aside_low, aside_high = lax.optimization_barrier((attach, aside_low, aside_high))
    beside_low = rolled(attach[:, -REACH:], 0, 1)
    beside_high = rolled(attach[:, :REACH], 0, -1)
    turn_down, turn_up = turns(
        aside_low, aside_high, side_low, side_high, attach, beside_low, beside_high
    )
    turn_low, turn_high = rolled(turn_up, 1, 0), rolled(turn_down, -1, 0)
    return deposit, transported(
        own, velocity, out_low, out_high, aside_low, aside_high,
        wide_low, wide_high, side_low, side_high, turn_low, turn_high,
        attach_rate, attach, beside_low, beside_high,
    )


def solution(mesh):
    return jax.shard_map(
        body,
        mesh=mesh,
        in_specs=(
            P(None, "wide", "narrow", None),
            P(None, "wide", "narrow", None),
            P(),
            P(("wide", "narrow"), None, None),
            P(("wide", "narrow"), None),
            P(("wide", "narrow"), None),
            P(("wide", "narrow"), None),
            P(("wide", "narrow"), None),
            P(("wide", "narrow"), None),
        ),
        out_specs=(P(None, "wide", "narrow", None), P(None, "wide", "narrow", None)),
        check_vma=False,
    )
```

time: 106 us -> 106 us (level)
  waiting for transfers between devices: 28.8 us -> 18.9 us
  starting transfers between devices: 27.3 us -> 33.2 us
  Pallas kernels: 43.5 us -> 49.3 us
  local copies, waits for them, and re-layouts: 4.93 us -> 3.01 us
    ppermute x10 -> x12, waiting for transfers between devices: 28.8 us -> 12.1 us  [rolled(): return lax.ppermute(block, AXES, pairs)]
    pallas_call x2 -> x4, Pallas kernels: 9.11 us -> 20.1 us  [the longest x1 9.06 us: first_moved(): pl.pallas_call(first_kernel, out_shape=(jax.ShapeDtypeStruct((16, 16, 32,...]
    all_to_all x1, waiting for transfers between devices: 0.01 us -> 6.76 us  [body(): got = lax.all_to_all(sent, AXES, split_axis=0, concat_axis=0, tiled=True)]
    ppermute x10 -> x12, starting transfers between devices: 18 us -> 23.2 us  [rolled(): return lax.ppermute(block, AXES, pairs)]
    pallas_call x1, Pallas kernels: 22.6 us -> 17.9 us  [transported(): pl.pallas_call(transport_kernel, out_shape=jax.ShapeDtypeStruct((32, 16,...]
    unnamed x24 -> x26, local copies, waits for them, and re-layouts: 3.27 us -> 1.97 us
  transfers between devices with their start and end apart: 11 -> 13, of which waited for: 5 -> 5; matrix products, arithmetic and copies ran while one was open for 2% -> 1% of each run, Pallas kernels for 13% -> 25%
where the time goes in v2:
time: 106 us; the launch traced here: 105 us
  Pallas kernels  49.3 us (47%)
  starting transfers between devices  33.2 us (31%)
  waiting for transfers between devices  18.9 us (18%)
  local copies, waits for them, and re-layouts  3.01 us (3%)
    ppermute x12, starting transfers between devices, rolled(): return lax.ppermute(block, AXES, pairs)  23.2 us
    pallas_call x1, Pallas kernels, transported(): pl.pallas_call(transport_kernel, out_shape=jax.ShapeDtypeStruct((32, 16,...  17.9 us
    ppermute x12, waiting for transfers between devices, rolled(): return lax.ppermute(block, AXES, pairs)  12.1 us
    pallas_call x1, Pallas kernels, deposited(): pl.pallas_call(deposit_kernel, out_shape=(jax.ShapeDtypeStruct((2, 16, 16...  11.2 us
    all_to_all x1, starting transfers between devices, body(): got = lax.all_to_all(sent, AXES, split_axis=0, concat_axis=0, tiled=True)  10 us
    pallas_call x1, Pallas kernels, first_moved(): pl.pallas_call(first_kernel, out_shape=(jax.ShapeDtypeStruct((16, 16, 32,...  9.06 us
    all_to_all x1, waiting for transfers between devices, body(): got = lax.all_to_all(sent, AXES, split_axis=0, concat_axis=0, tiled=True)  6.76 us
    pallas_call x1, Pallas kernels, edges_of(): pl.pallas_call(edges_kernel, out_shape=(jax.ShapeDtypeStruct((16 + 2 * RE...  5.17 us
  transfers between devices with their start and end apart: 13, of which 5 were waited for; matrix products, arithmetic and copies ran while one was open for 1% of the time, Pallas kernels for 25%

profile of v2, /device:TPU:0, one launch (start us, length us, event | category | flops | bytes accessed | tf_op | source)
XLA Modules:
  0.0 105.1 jit_solution(1277844285476769309)
XLA Ops:
  0.6 5.2 %shard_map.104 = (f32[22,32,128]{2,1,0:T(8,128)}, f32[22,32,128]{2,1,0:T(8,128)}, f32[16,2,32,128]{3,2,1,0:T(8,128)}, f32[16,2,32,128]{3,2,1,0:T(8,128)}) custom-call(f32[32,16,16,128]{3,2,1,0:T(8,128)} %classes.3, f32[3,16,16,128]{3,2,1,0:T(8,128)} %velocity.5), custom_call_target="tpu_custom_call" | custom-call | tf_op jit(solution)/shard_map/pallas_call | solution.py:80
  5.8 0.0 collective-permute-start
  5.8 3.6 %collective-permute-start.1 = (f32[16,2,32,128]{3,2,1,0:T(8,128)}, f32[16,2,32,128]{3,2,1,0:T(8,128)S(1)}, u32[]{:S(2)}, u32[]{:S(2)}) collective-permute-start(f32[16,2,32,128]{3,2,1,0:T(8,128)} %get-tuple-element.40), channel_id=1, source_target_pairs={{0,7},{1,0},{2,1},{3,2},{4,3},{5,4},{6,5},{7,6},{8,15},{9,8},{10,9... | collective-permute-start | bytes 1572872 | tf_op jit(solution)/shard_map/ppermute | solution.py:34
  9.4 1.6 %collective-permute-start.2 = (f32[22,32,128]{2,1,0:T(8,128)}, f32[22,32,128]{2,1,0:T(8,128)S(1)}, u32[]{:S(2)}, u32[]{:S(2)}) collective-permute-start(f32[22,32,128]{2,1,0:T(8,128)} %get-tuple-element.41), channel_id=1, source_target_pairs={{0,8},{1,9},{2,10},{3,11},{4,12},{5,13},{6,14},{7,15},{8,16},{9,17... | collective-permute-start | bytes 1081352 | tf_op jit(solution)/shard_map/ppermute | solution.py:34
  11.0 3.8 %collective-permute-start.3 = (f32[22,32,128]{2,1,0:T(8,128)}, f32[22,32,128]{2,1,0:T(8,128)S(1)}, u32[]{:S(2)}, u32[]{:S(2)}) collective-permute-start(f32[22,32,128]{2,1,0:T(8,128)} %get-tuple-element.42), channel_id=1, source_target_pairs={{0,120},{1,121},{2,122},{3,123},{4,124},{5,125},{6,126},{7,127},{8... | collective-permute-start | bytes 1081352 | tf_op jit(solution)/shard_map/ppermute | solution.py:34
  14.7 3.2 %shard_map.105 = f32[128,1,1408]{2,1,0:T(1,128)} custom-call(s32[1,96]{1,0:T(1,128)} %bitcast.7, s32[8,12]{1,0:T(8,128)} %bitcast.5, s32[2,96]{1,0:T(2,128)} %bitcast.6, f32[3,96,128]{2,1,0:T(8,128)} %bitcast.4, f32[96,128]{1,0:T(8,128)} %volume, f32[96,128]{1,0:T(8,128)} %area.1), custom_call_target="tpu_custom_call" | custom-call | tf_op jit(solution)/shard_map/pallas_call | solution.py:139
  17.9 4.0 %collective-permute-done.2.wide_low = f32[22,32,128]{2,1,0:T(8,128)S(1)} collective-permute-done((f32[22,32,128]{2,1,0:T(8,128)}, f32[22,32,128]{2,1,0:T(8,128)S(1)}, u32[]{:S(2)}, u32[]{:S(2)}) %collective-permute-start.2) | collective-permute-done | bytes 360480 | tf_op jit(solution)/shard_map/ppermute | solution.py:34
  21.9 0.0 collective-permute-done.3.wide_high
  21.9 0.0 collective-permute-done.side_low
  21.9 0.0 copy-start.1
  22.0 0.0 collective-permute-done.1.side_high
  22.0 0.0 copy-start.2
  22.0 10.0 %all-to-all-start = ((f32[128,1,1408]{2,1,0:T(1,128)}), f32[128,1,1408]{2,1,0:T(1,128)S(1)}, u32[]{:S(2)}, u32[]{:S(2)}) async-start(f32[128,1,1408]{2,1,0:T(1,128)} %shard_map.105), calls=%async_computation | async-start | bytes 1441792 | tf_op jit(solution)/shard_map/all_to_all | solution.py:657
  32.0 0.0 copy-done.5
  32.0 0.0 copy-done.6
  32.0 0.0 copy-done.1
  32.0 0.0 copy-done.2
  32.0 9.1 %shard_map.106 = (f32[16,16,32,128]{3,2,1,0:T(8,128)}, f32[3,16,32,128]{3,2,1,0:T(8,128)}, f32[3,16,32,128]{3,2,1,0:T(8,128)}, f32[16,3,32,128]{3,2,1,0:T(8,128)}, f32[16,3,32,128]{3,2,1,0:T(8,128)}) custom-call(f32[32,16,16,128]{3,2,1,0:T(8,128)} %classes.3, f32[3,16,16,128]{3,2,1,0:T(8,128)} %velocity.5, f32[22,32,128]{2,1,0:T(8,128)} %copy-done.5, ...), custom_call_target="tpu_custom_call" | custom-call | tf_op jit(solution)/shard_map/pallas_call | solution.py:394
  41.1 6.8 %all-to-all-done.got_any.got = f32[128,1,1408]{2,1,0:T(1,128)S(1)} async-done(((f32[128,1,1408]{2,1,0:T(1,128)}), f32[128,1,1408]{2,1,0:T(1,128)S(1)}, u32[]{:S(2)}, u32[]{:S(2)}) %all-to-all-start) | async-done | bytes 720928 | tf_op jit(solution)/shard_map/all_to_all | solution.py:657
  47.9 0.0 collective-permute-start.6
  47.9 3.0 %collective-permute-start.7 = (f32[16,3,32,128]{3,2,1,0:T(8,128)}, f32[16,3,32,128]{3,2,1,0:T(8,128)S(1)}, u32[]{:S(2)}, u32[]{:S(2)}) collective-permute-start(f32[16,3,32,128]{3,2,1,0:T(8,128)} %get-tuple-element.60), channel_id=1, source_target_pairs={{0,7},{1,0},{2,1},{3,2},{4,3},{5,4},{6,5},{7,6},{8,15},{9,8},{10,9... | collective-permute-start | bytes 2359304 | tf_op jit(solution)/shard_map/ppermute | solution.py:34
  50.8 0.6 collective-permute-start.4
  51.4 4.8 %collective-permute-start.5 = (f32[3,16,32,128]{3,2,1,0:T(8,128)}, f32[3,16,32,128]{3,2,1,0:T(8,128)S(1)}, u32[]{:S(2)}, u32[]{:S(2)}) collective-permute-start(f32[3,16,32,128]{3,2,1,0:T(8,128)} %get-tuple-element.57), channel_id=1, source_target_pairs={{0,120},{1,121},{2,122},{3,123},{4,124},{5,125},{6,126},{7,127},{8... | collective-permute-start | bytes 2359304 | tf_op jit(solution)/shard_map/ppermute | solution.py:34
  56.2 0.0 copy-done
  56.2 11.2 %shard_map.107 = (f32[2,16,16,128]{3,2,1,0:T(8,128)}, f32[16,16,128]{2,1,0:T(8,128)}) custom-call(f32[128,1,1408]{2,1,0:T(1,128)} %copy-done, f32[128,1,1408]{2,1,0:T(1,128)} %copy-done), custom_call_target="tpu_custom_call" | custom-call | tf_op jit(solution)/shard_map/pallas_call | solution.py:226
  67.3 0.0 collective-permute-done.6.aside_low
  67.4 0.0 copy-start.3
  67.4 0.0 collective-permute-done.7.aside_high
  67.4 0.0 copy-start.4
  67.4 1.0 fusion
  68.4 0.0 collective-permute-start.9
  68.5 0.5 collective-permute-start.8
  69.0 1.1 %collective-permute-done.9.beside_high = f32[16,3,128]{2,1,0:T(4,128)S(1)} collective-permute-done((f32[16,3,128]{2,1,0:T(4,128)S(1)}, f32[16,3,128]{2,1,0:T(4,128)S(1)}, u32[]{:S(2)}, u32[]{:S(2)}) %collective-permute-start.9) | collective-permute-done | bytes 24608 | tf_op jit(solution)/shard_map/ppermute | solution.py:34
  70.1 3.0 %collective-permute-done.8.beside_low = f32[16,3,128]{2,1,0:T(4,128)S(1)} collective-permute-done((f32[16,3,128]{2,1,0:T(4,128)S(1)}, f32[16,3,128]{2,1,0:T(4,128)S(1)}, u32[]{:S(2)}, u32[]{:S(2)}) %collective-permute-start.8) | collective-permute-done | bytes 24608 | tf_op jit(solution)/shard_map/ppermute | solution.py:34
  73.0 0.0 copy-done.3
  73.0 0.0 copy-done.11
  73.0 0.6 copy-done.12
  73.6 2.7 %shard_map.108 = (f32[13,32,128]{2,1,0:T(8,128)}, f32[13,32,128]{2,1,0:T(8,128)}) custom-call(f32[16,3,32,128]{3,2,1,0:T(8,128)} %copy-done.3, f32[16,3,32,128]{3,2,1,0:T(8,128)} %copy-done.4, f32[16,2,32,128]{3,2,1,0:T(8,128)} %copy-done.1, f32[16,2,32,128]{3,2,1,0:T(8,128)} %copy-done.2, f32[16,16,128]{2,1,0:T(8,128)} %get-tuple-element.63.attach, ...), custom_call_target="tpu_custom_call" | custom-call | tf_op jit(solution)/shard_map/pallas_call | solution.py:447
  76.4 0.1 collective-permute-start.10
  76.5 5.3 %collective-permute-start.11 = (f32[13,32,128]{2,1,0:T(8,128)}, f32[13,32,128]{2,1,0:T(8,128)S(1)}, u32[]{:S(2)}, u32[]{:S(2)}) collective-permute-start(f32[13,32,128]{2,1,0:T(8,128)} %get-tuple-element.65), channel_id=1, source_target_pairs={{0,120},{1,121},{2,122},{3,123},{4,124},{5,125},{6,126},{7,127},{8... | collective-permute-start | bytes 638984 | tf_op jit(solution)/shard_map/ppermute | solution.py:34
  81.8 0.0 collective-permute-done.4.out_low
  81.8 0.0 collective-permute-done.5.out_high
  81.8 0.0 copy-start.8
  81.8 4.0 %collective-permute-done.10.turn_low = f32[13,32,128]{2,1,0:T(8,128)S(1)} collective-permute-done((f32[13,32,128]{2,1,0:T(8,128)}, f32[13,32,128]{2,1,0:T(8,128)S(1)}, u32[]{:S(2)}, u32[]{:S(2)}) %collective-permute-start.10) | collective-permute-done | bytes 213024 | tf_op jit(solution)/shard_map/ppermute | solution.py:34
  85.8 0.0 collective-permute-done.11.turn_high
  85.8 0.7 copy-done.9
  86.5 0.7 copy-done.10
  87.2 17.9 %shard_map.109 = f32[32,16,16,128]{3,2,1,0:T(8,128)} custom-call(f32[16,16,32,128]{3,2,1,0:T(8,128)} %get-tuple-element.55.own, f32[3,16,16,128]{3,2,1,0:T(8,128)} %velocity.5, f32[3,16,32,128]{3,2,1,0:T(8,128)} %copy-done.7, f32[3,16,32,128]{3,2,1,0:T(8,128)} %copy-done.8, f32[16,3,32,128]{3,2,1,0:T(8,128)} %copy-done.3, f32[16,3,32,128]{3,2,1,0:T(8,128)} %copy-done.4, ...), custom_call_target="tpu_custom_call" | custom-call | tf_op jit(solution)/shard_map/pallas_call | solution.py:609
  (11 shorter events, 0.0 us)
Async XLA Ops:
  5.8 16.1 %collective-permute-start = (f32[16,2,32,128]{3,2,1,0:T(8,128)}, f32[16,2,32,128]{3,2,1,0:T(8,128)S(1)}, u32[]{:S(2)}, u32[]{:S(2)}) collective-permute-start(f32[16,2,32,128]{3,2,1,0:T(8,128)} %get-tuple-element.39), channel_id=1, source_target_pairs={{0,1},{1,2},{2,3},{3,4},{4,5},{5,6},{6,7},{7,0},{8,9},{9,10},{10,1... | collective-permute-start | bytes 1572872 | tf_op jit(solution)/shard_map/ppermute | solution.py:34
  5.8 16.1 %collective-permute-start.1 = (f32[16,2,32,128]{3,2,1,0:T(8,128)}, f32[16,2,32,128]{3,2,1,0:T(8,128)S(1)}, u32[]{:S(2)}, u32[]{:S(2)}) collective-permute-start(f32[16,2,32,128]{3,2,1,0:T(8,128)} %get-tuple-element.40), channel_id=1, source_target_pairs={{0,7},{1,0},{2,1},{3,2},{4,3},{5,4},{6,5},{7,6},{8,15},{9,8},{10,9... | collective-permute-start | bytes 1572872 | tf_op jit(solution)/shard_map/ppermute | solution.py:34
  9.4 12.5 %collective-permute-start.2 = (f32[22,32,128]{2,1,0:T(8,128)}, f32[22,32,128]{2,1,0:T(8,128)S(1)}, u32[]{:S(2)}, u32[]{:S(2)}) collective-permute-start(f32[22,32,128]{2,1,0:T(8,128)} %get-tuple-element.41), channel_id=1, source_target_pairs={{0,8},{1,9},{2,10},{3,11},{4,12},{5,13},{6,14},{7,15},{8,16},{9,17... | collective-permute-start | bytes 1081352 | tf_op jit(solution)/shard_map/ppermute | solution.py:34
  11.0 11.0 %collective-permute-start.3 = (f32[22,32,128]{2,1,0:T(8,128)}, f32[22,32,128]{2,1,0:T(8,128)S(1)}, u32[]{:S(2)}, u32[]{:S(2)}) collective-permute-start(f32[22,32,128]{2,1,0:T(8,128)} %get-tuple-element.42), channel_id=1, source_target_pairs={{0,120},{1,121},{2,122},{3,123},{4,124},{5,125},{6,126},{7,127},{8... | collective-permute-start | bytes 1081352 | tf_op jit(solution)/shard_map/ppermute | solution.py:34
  21.9 10.1 %copy-start.5 = (f32[22,32,128]{2,1,0:T(8,128)}, f32[22,32,128]{2,1,0:T(8,128)S(1)}, u32[]{:S(2)}) copy-start(f32[22,32,128]{2,1,0:T(8,128)S(1)} %collective-permute-done.2.wide_low) | copy-start | bytes 1081348
  21.9 10.1 %copy-start.6 = (f32[22,32,128]{2,1,0:T(8,128)}, f32[22,32,128]{2,1,0:T(8,128)S(1)}, u32[]{:S(2)}) copy-start(f32[22,32,128]{2,1,0:T(8,128)S(1)} %collective-permute-done.3.wide_high) | copy-start | bytes 1081348
  21.9 10.1 %copy-start.1 = (f32[16,2,32,128]{3,2,1,0:T(8,128)}, f32[16,2,32,128]{3,2,1,0:T(8,128)S(1)}, u32[]{:S(2)}) copy-start(f32[16,2,32,128]{3,2,1,0:T(8,128)S(1)} %collective-permute-done.side_low) | copy-start | bytes 1572868
  22.0 10.1 %copy-start.2 = (f32[16,2,32,128]{3,2,1,0:T(8,128)}, f32[16,2,32,128]{3,2,1,0:T(8,128)S(1)}, u32[]{:S(2)}) copy-start(f32[16,2,32,128]{3,2,1,0:T(8,128)S(1)} %collective-permute-done.1.side_high) | copy-start | bytes 1572868
  22.0 25.9 %all-to-all-start = ((f32[128,1,1408]{2,1,0:T(1,128)}), f32[128,1,1408]{2,1,0:T(1,128)S(1)}, u32[]{:S(2)}, u32[]{:S(2)}) async-start(f32[128,1,1408]{2,1,0:T(1,128)} %shard_map.105), calls=%async_computation | async-start | bytes 1441792 | tf_op jit(solution)/shard_map/all_to_all | solution.py:657
  47.8 8.3 %copy-start = (f32[128,1,1408]{2,1,0:T(1,128)}, f32[128,1,1408]{2,1,0:T(1,128)S(1)}, u32[]{:S(2)}) copy-start(f32[128,1,1408]{2,1,0:T(1,128)S(1)} %all-to-all-done.got_any.got) | copy-start | bytes 2162692
  47.9 19.5 %collective-permute-start.6 = (f32[16,3,32,128]{3,2,1,0:T(8,128)}, f32[16,3,32,128]{3,2,1,0:T(8,128)S(1)}, u32[]{:S(2)}, u32[]{:S(2)}) collective-permute-start(f32[16,3,32,128]{3,2,1,0:T(8,128)} %get-tuple-element.59), channel_id=1, source_target_pairs={{0,1},{1,2},{2,3},{3,4},{4,5},{5,6},{6,7},{7,0},{8,9},{9,10},{10,1... | collective-permute-start | bytes 2359304 | tf_op jit(solution)/shard_map/ppermute | solution.py:34
  47.9 19.5 %collective-permute-start.7 = (f32[16,3,32,128]{3,2,1,0:T(8,128)}, f32[16,3,32,128]{3,2,1,0:T(8,128)S(1)}, u32[]{:S(2)}, u32[]{:S(2)}) collective-permute-start(f32[16,3,32,128]{3,2,1,0:T(8,128)} %get-tuple-element.60), channel_id=1, source_target_pairs={{0,7},{1,0},{2,1},{3,2},{4,3},{5,4},{6,5},{7,6},{8,15},{9,8},{10,9... | collective-permute-start | bytes 2359304 | tf_op jit(solution)/shard_map/ppermute | solution.py:34
  50.8 31.0 %collective-permute-start.4 = (f32[3,16,32,128]{3,2,1,0:T(8,128)}, f32[3,16,32,128]{3,2,1,0:T(8,128)S(1)}, u32[]{:S(2)}, u32[]{:S(2)}) collective-permute-start(f32[3,16,32,128]{3,2,1,0:T(8,128)} %get-tuple-element.56), channel_id=1, source_target_pairs={{0,8},{1,9},{2,10},{3,11},{4,12},{5,13},{6,14},{7,15},{8,16},{9,17... | collective-permute-start | bytes 2359304 | tf_op jit(solution)/shard_map/ppermute | solution.py:34
  51.4 30.4 %collective-permute-start.5 = (f32[3,16,32,128]{3,2,1,0:T(8,128)}, f32[3,16,32,128]{3,2,1,0:T(8,128)S(1)}, u32[]{:S(2)}, u32[]{:S(2)}) collective-permute-start(f32[3,16,32,128]{3,2,1,0:T(8,128)} %get-tuple-element.57), channel_id=1, source_target_pairs={{0,120},{1,121},{2,122},{3,123},{4,124},{5,125},{6,126},{7,127},{8... | collective-permute-start | bytes 2359304 | tf_op jit(solution)/shard_map/ppermute | solution.py:34
  67.4 5.7 %copy-start.3 = (f32[16,3,32,128]{3,2,1,0:T(8,128)}, f32[16,3,32,128]{3,2,1,0:T(8,128)S(1)}, u32[]{:S(2)}) copy-start(f32[16,3,32,128]{3,2,1,0:T(8,128)S(1)} %collective-permute-done.6.aside_low) | copy-start | bytes 2359300
  67.4 5.6 %copy-start.4 = (f32[16,3,32,128]{3,2,1,0:T(8,128)}, f32[16,3,32,128]{3,2,1,0:T(8,128)S(1)}, u32[]{:S(2)}) copy-start(f32[16,3,32,128]{3,2,1,0:T(8,128)S(1)} %collective-permute-done.7.aside_high) | copy-start | bytes 2359300
  68.4 1.6 %collective-permute-start.9 = (f32[16,3,128]{2,1,0:T(4,128)S(1)}, f32[16,3,128]{2,1,0:T(4,128)S(1)}, u32[]{:S(2)}, u32[]{:S(2)}) collective-permute-start(f32[16,3,128]{2,1,0:T(4,128)S(1)} %get-tuple-element.66), channel_id=1, source_target_pairs={{0,7},{1,0},{2,1},{3,2},{4,3},{5,4},{6,5},{7,6},{8,15},{9,8},{10,9... | collective-permute-start | bytes 73736 | tf_op jit(solution)/shard_map/ppermute | solution.py:34
  68.5 4.6 %collective-permute-start.8 = (f32[16,3,128]{2,1,0:T(4,128)S(1)}, f32[16,3,128]{2,1,0:T(4,128)S(1)}, u32[]{:S(2)}, u32[]{:S(2)}) collective-permute-start(f32[16,3,128]{2,1,0:T(4,128)S(1)} %get-tuple-element.67), channel_id=1, source_target_pairs={{0,1},{1,2},{2,3},{3,4},{4,5},{5,6},{6,7},{7,0},{8,9},{9,10},{10,1... | collective-permute-start | bytes 73736 | tf_op jit(solution)/shard_map/ppermute | solution.py:34
  70.1 3.0 %copy-start.11 = (f32[16,3,128]{2,1,0:T(4,128)}, f32[16,3,128]{2,1,0:T(4,128)S(1)}, u32[]{:S(2)}) copy-start(f32[16,3,128]{2,1,0:T(4,128)S(1)} %collective-permute-done.9.beside_high) | copy-start | bytes 73732
  73.0 0.6 copy-start.12
  76.4 9.4 %collective-permute-start.10 = (f32[13,32,128]{2,1,0:T(8,128)}, f32[13,32,128]{2,1,0:T(8,128)S(1)}, u32[]{:S(2)}, u32[]{:S(2)}) collective-permute-start(f32[13,32,128]{2,1,0:T(8,128)} %get-tuple-element.64), channel_id=1, source_target_pairs={{0,8},{1,9},{2,10},{3,11},{4,12},{5,13},{6,14},{7,15},{8,16},{9,17... | collective-permute-start | bytes 638984 | tf_op jit(solution)/shard_map/ppermute | solution.py:34
  76.5 9.4 %collective-permute-start.11 = (f32[13,32,128]{2,1,0:T(8,128)}, f32[13,32,128]{2,1,0:T(8,128)S(1)}, u32[]{:S(2)}, u32[]{:S(2)}) collective-permute-start(f32[13,32,128]{2,1,0:T(8,128)} %get-tuple-element.65), channel_id=1, source_target_pairs={{0,120},{1,121},{2,122},{3,123},{4,124},{5,125},{6,126},{7,127},{8... | collective-permute-start | bytes 638984 | tf_op jit(solution)/shard_map/ppermute | solution.py:34
  81.8 4.0 %copy-start.7 = (f32[3,16,32,128]{3,2,1,0:T(8,128)}, f32[3,16,32,128]{3,2,1,0:T(8,128)S(1)}, u32[]{:S(2)}) copy-start(f32[3,16,32,128]{3,2,1,0:T(8,128)S(1)} %collective-permute-done.4.out_low) | copy-start | bytes 2359300
  81.8 4.0 %copy-start.8 = (f32[3,16,32,128]{3,2,1,0:T(8,128)}, f32[3,16,32,128]{3,2,1,0:T(8,128)S(1)}, u32[]{:S(2)}) copy-start(f32[3,16,32,128]{3,2,1,0:T(8,128)S(1)} %collective-permute-done.5.out_high) | copy-start | bytes 2359300
  85.8 0.7 copy-start.9
  86.5 0.7 copy-start.10

commit v3 on v2

--- a/solution.py
+++ b/solution.py
@@ -235,7 +235,7 @@
         ],
         out_specs=(pl.BlockSpec(memory_space=pltpu.VMEM),) * 2,
         scratch_shapes=[
-            pltpu.VMEM((512, 128), jnp.float32),
+            pltpu.VMEM((520, 128), jnp.float32),
             pltpu.SMEM((devices, 1, 128), jnp.float32),
             pltpu.SemaphoreType.DMA,
         ],

time: 106 us -> 106 us (level)
  no operation moved by 1% of the time
where the time goes in v3:
time: 106 us; the launch traced here: 105 us
  Pallas kernels  49.3 us (47%)
  starting transfers between devices  33.2 us (31%)
  waiting for transfers between devices  18.9 us (18%)
  local copies, waits for them, and re-layouts  3.01 us (3%)
    ppermute x12, starting transfers between devices, rolled(): return lax.ppermute(block, AXES, pairs)  23.2 us
    pallas_call x1, Pallas kernels, transported(): pl.pallas_call(transport_kernel, out_shape=jax.ShapeDtypeStruct((32, 16,...  17.9 us
    ppermute x12, waiting for transfers between devices, rolled(): return lax.ppermute(block, AXES, pairs)  12.1 us
    pallas_call x1, Pallas kernels, deposited(): pl.pallas_call(deposit_kernel, out_shape=(jax.ShapeDtypeStruct((2, 16, 16...  11.2 us
    all_to_all x1, starting transfers between devices, body(): got = lax.all_to_all(sent, AXES, split_axis=0, concat_axis=0, tiled=True)  10 us
    pallas_call x1, Pallas kernels, first_moved(): pl.pallas_call(first_kernel, out_shape=(jax.ShapeDtypeStruct((16, 16, 32,...  9.06 us
    all_to_all x1, waiting for transfers between devices, body(): got = lax.all_to_all(sent, AXES, split_axis=0, concat_axis=0, tiled=True)  6.76 us
    pallas_call x1, Pallas kernels, edges_of(): pl.pallas_call(edges_kernel, out_shape=(jax.ShapeDtypeStruct((16 + 2 * RE...  5.17 us
  transfers between devices with their start and end apart: 13, of which 5 were waited for; matrix products, arithmetic and copies ran while one was open for 1% of the time, Pallas kernels for 25%

profile of v3, /device:TPU:0, one launch (start us, length us, event | category | flops | bytes accessed | tf_op | source)
XLA Modules:
  0.0 105.2 jit_solution(15920640873756418666)
XLA Ops:
  0.6 5.2 %shard_map.104 = (f32[22,32,128]{2,1,0:T(8,128)}, f32[22,32,128]{2,1,0:T(8,128)}, f32[16,2,32,128]{3,2,1,0:T(8,128)}, f32[16,2,32,128]{3,2,1,0:T(8,128)}) custom-call(f32[32,16,16,128]{3,2,1,0:T(8,128)} %classes.3, f32[3,16,16,128]{3,2,1,0:T(8,128)} %velocity.5), custom_call_target="tpu_custom_call" | custom-call | tf_op jit(solution)/shard_map/pallas_call | solution.py:80
  5.8 0.0 collective-permute-start
  5.8 3.6 %collective-permute-start.1 = (f32[16,2,32,128]{3,2,1,0:T(8,128)}, f32[16,2,32,128]{3,2,1,0:T(8,128)S(1)}, u32[]{:S(2)}, u32[]{:S(2)}) collective-permute-start(f32[16,2,32,128]{3,2,1,0:T(8,128)} %get-tuple-element.40), channel_id=1, source_target_pairs={{0,7},{1,0},{2,1},{3,2},{4,3},{5,4},{6,5},{7,6},{8,15},{9,8},{10,9... | collective-permute-start | bytes 1572872 | tf_op jit(solution)/shard_map/ppermute | solution.py:34
  9.4 1.6 %collective-permute-start.2 = (f32[22,32,128]{2,1,0:T(8,128)}, f32[22,32,128]{2,1,0:T(8,128)S(1)}, u32[]{:S(2)}, u32[]{:S(2)}) collective-permute-start(f32[22,32,128]{2,1,0:T(8,128)} %get-tuple-element.41), channel_id=1, source_target_pairs={{0,8},{1,9},{2,10},{3,11},{4,12},{5,13},{6,14},{7,15},{8,16},{9,17... | collective-permute-start | bytes 1081352 | tf_op jit(solution)/shard_map/ppermute | solution.py:34
  11.0 3.8 %collective-permute-start.3 = (f32[22,32,128]{2,1,0:T(8,128)}, f32[22,32,128]{2,1,0:T(8,128)S(1)}, u32[]{:S(2)}, u32[]{:S(2)}) collective-permute-start(f32[22,32,128]{2,1,0:T(8,128)} %get-tuple-element.42), channel_id=1, source_target_pairs={{0,120},{1,121},{2,122},{3,123},{4,124},{5,125},{6,126},{7,127},{8... | collective-permute-start | bytes 1081352 | tf_op jit(solution)/shard_map/ppermute | solution.py:34
  14.7 3.2 %shard_map.105 = f32[128,1,1408]{2,1,0:T(1,128)} custom-call(s32[1,96]{1,0:T(1,128)} %bitcast.7, s32[8,12]{1,0:T(8,128)} %bitcast.5, s32[2,96]{1,0:T(2,128)} %bitcast.6, f32[3,96,128]{2,1,0:T(8,128)} %bitcast.4, f32[96,128]{1,0:T(8,128)} %volume, f32[96,128]{1,0:T(8,128)} %area.1), custom_call_target="tpu_custom_call" | custom-call | tf_op jit(solution)/shard_map/pallas_call | solution.py:139
  17.9 4.0 %collective-permute-done.2.wide_low = f32[22,32,128]{2,1,0:T(8,128)S(1)} collective-permute-done((f32[22,32,128]{2,1,0:T(8,128)}, f32[22,32,128]{2,1,0:T(8,128)S(1)}, u32[]{:S(2)}, u32[]{:S(2)}) %collective-permute-start.2) | collective-permute-done | bytes 360480 | tf_op jit(solution)/shard_map/ppermute | solution.py:34
  21.9 0.0 collective-permute-done.3.wide_high
  21.9 0.0 collective-permute-done.side_low
  21.9 0.0 copy-start.1
  22.0 0.0 collective-permute-done.1.side_high
  22.0 0.0 copy-start.2
  22.0 10.0 %all-to-all-start = ((f32[128,1,1408]{2,1,0:T(1,128)}), f32[128,1,1408]{2,1,0:T(1,128)S(1)}, u32[]{:S(2)}, u32[]{:S(2)}) async-start(f32[128,1,1408]{2,1,0:T(1,128)} %shard_map.105), calls=%async_computation | async-start | bytes 1441792 | tf_op jit(solution)/shard_map/all_to_all | solution.py:657
  32.0 0.0 copy-done.5
  32.0 0.0 copy-done.6
  32.0 0.0 copy-done.1
  32.0 0.0 copy-done.2
  32.0 9.1 %shard_map.106 = (f32[16,16,32,128]{3,2,1,0:T(8,128)}, f32[3,16,32,128]{3,2,1,0:T(8,128)}, f32[3,16,32,128]{3,2,1,0:T(8,128)}, f32[16,3,32,128]{3,2,1,0:T(8,128)}, f32[16,3,32,128]{3,2,1,0:T(8,128)}) custom-call(f32[32,16,16,128]{3,2,1,0:T(8,128)} %classes.3, f32[3,16,16,128]{3,2,1,0:T(8,128)} %velocity.5, f32[22,32,128]{2,1,0:T(8,128)} %copy-done.5, ...), custom_call_target="tpu_custom_call" | custom-call | tf_op jit(solution)/shard_map/pallas_call | solution.py:394
  41.1 6.8 %all-to-all-done.got_any.got = f32[128,1,1408]{2,1,0:T(1,128)S(1)} async-done(((f32[128,1,1408]{2,1,0:T(1,128)}), f32[128,1,1408]{2,1,0:T(1,128)S(1)}, u32[]{:S(2)}, u32[]{:S(2)}) %all-to-all-start) | async-done | bytes 720928 | tf_op jit(solution)/shard_map/all_to_all | solution.py:657
  47.9 0.0 collective-permute-start.6
  47.9 3.0 %collective-permute-start.7 = (f32[16,3,32,128]{3,2,1,0:T(8,128)}, f32[16,3,32,128]{3,2,1,0:T(8,128)S(1)}, u32[]{:S(2)}, u32[]{:S(2)}) collective-permute-start(f32[16,3,32,128]{3,2,1,0:T(8,128)} %get-tuple-element.60), channel_id=1, source_target_pairs={{0,7},{1,0},{2,1},{3,2},{4,3},{5,4},{6,5},{7,6},{8,15},{9,8},{10,9... | collective-permute-start | bytes 2359304 | tf_op jit(solution)/shard_map/ppermute | solution.py:34
  50.8 0.6 collective-permute-start.4
  51.4 4.8 %collective-permute-start.5 = (f32[3,16,32,128]{3,2,1,0:T(8,128)}, f32[3,16,32,128]{3,2,1,0:T(8,128)S(1)}, u32[]{:S(2)}, u32[]{:S(2)}) collective-permute-start(f32[3,16,32,128]{3,2,1,0:T(8,128)} %get-tuple-element.57), channel_id=1, source_target_pairs={{0,120},{1,121},{2,122},{3,123},{4,124},{5,125},{6,126},{7,127},{8... | collective-permute-start | bytes 2359304 | tf_op jit(solution)/shard_map/ppermute | solution.py:34
  56.2 0.0 copy-done
  56.2 11.2 %shard_map.107 = (f32[2,16,16,128]{3,2,1,0:T(8,128)}, f32[16,16,128]{2,1,0:T(8,128)}) custom-call(f32[128,1,1408]{2,1,0:T(1,128)} %copy-done, f32[128,1,1408]{2,1,0:T(1,128)} %copy-done), custom_call_target="tpu_custom_call" | custom-call | tf_op jit(solution)/shard_map/pallas_call | solution.py:226
  67.4 0.0 collective-permute-done.6.aside_low
  67.4 0.0 copy-start.3
  67.4 0.0 collective-permute-done.7.aside_high
  67.4 0.0 copy-start.4
  67.4 1.0 fusion
  68.5 0.0 collective-permute-start.9
  68.5 0.5 collective-permute-start.8
  69.0 1.1 %collective-permute-done.9.beside_high = f32[16,3,128]{2,1,0:T(4,128)S(1)} collective-permute-done((f32[16,3,128]{2,1,0:T(4,128)S(1)}, f32[16,3,128]{2,1,0:T(4,128)S(1)}, u32[]{:S(2)}, u32[]{:S(2)}) %collective-permute-start.9) | collective-permute-done | bytes 24608 | tf_op jit(solution)/shard_map/ppermute | solution.py:34
  70.1 3.0 %collective-permute-done.8.beside_low = f32[16,3,128]{2,1,0:T(4,128)S(1)} collective-permute-done((f32[16,3,128]{2,1,0:T(4,128)S(1)}, f32[16,3,128]{2,1,0:T(4,128)S(1)}, u32[]{:S(2)}, u32[]{:S(2)}) %collective-permute-start.8) | collective-permute-done | bytes 24608 | tf_op jit(solution)/shard_map/ppermute | solution.py:34
  73.1 0.0 copy-done.3
  73.1 0.6 copy-done.12
  73.7 2.7 %shard_map.108 = (f32[13,32,128]{2,1,0:T(8,128)}, f32[13,32,128]{2,1,0:T(8,128)}) custom-call(f32[16,3,32,128]{3,2,1,0:T(8,128)} %copy-done.3, f32[16,3,32,128]{3,2,1,0:T(8,128)} %copy-done.4, f32[16,2,32,128]{3,2,1,0:T(8,128)} %copy-done.1, f32[16,2,32,128]{3,2,1,0:T(8,128)} %copy-done.2, f32[16,16,128]{2,1,0:T(8,128)} %get-tuple-element.63.attach, ...), custom_call_target="tpu_custom_call" | custom-call | tf_op jit(solution)/shard_map/pallas_call | solution.py:447
  76.4 0.1 collective-permute-start.10
  76.5 5.3 %collective-permute-start.11 = (f32[13,32,128]{2,1,0:T(8,128)}, f32[13,32,128]{2,1,0:T(8,128)S(1)}, u32[]{:S(2)}, u32[]{:S(2)}) collective-permute-start(f32[13,32,128]{2,1,0:T(8,128)} %get-tuple-element.65), channel_id=1, source_target_pairs={{0,120},{1,121},{2,122},{3,123},{4,124},{5,125},{6,126},{7,127},{8... | collective-permute-start | bytes 638984 | tf_op jit(solution)/shard_map/ppermute | solution.py:34
  81.9 0.0 collective-permute-done.4.out_low
  81.9 0.0 collective-permute-done.5.out_high
  81.9 4.0 %collective-permute-done.10.turn_low = f32[13,32,128]{2,1,0:T(8,128)S(1)} collective-permute-done((f32[13,32,128]{2,1,0:T(8,128)}, f32[13,32,128]{2,1,0:T(8,128)S(1)}, u32[]{:S(2)}, u32[]{:S(2)}) %collective-permute-start.10) | collective-permute-done | bytes 213024 | tf_op jit(solution)/shard_map/ppermute | solution.py:34
  85.9 0.0 collective-permute-done.11.turn_high
  85.9 0.0 copy-done.7
  85.9 0.0 copy-done.8
  85.9 0.7 copy-done.9
  86.6 0.7 copy-done.10
  87.2 17.9 %shard_map.109 = f32[32,16,16,128]{3,2,1,0:T(8,128)} custom-call(f32[16,16,32,128]{3,2,1,0:T(8,128)} %get-tuple-element.55.own, f32[3,16,16,128]{3,2,1,0:T(8,128)} %velocity.5, f32[3,16,32,128]{3,2,1,0:T(8,128)} %copy-done.7, f32[3,16,32,128]{3,2,1,0:T(8,128)} %copy-done.8, f32[16,3,32,128]{3,2,1,0:T(8,128)} %copy-done.3, f32[16,3,32,128]{3,2,1,0:T(8,128)} %copy-done.4, ...), custom_call_target="tpu_custom_call" | custom-call | tf_op jit(solution)/shard_map/pallas_call | solution.py:609
  (11 shorter events, 0.0 us)
Async XLA Ops:
  5.8 16.1 %collective-permute-start = (f32[16,2,32,128]{3,2,1,0:T(8,128)}, f32[16,2,32,128]{3,2,1,0:T(8,128)S(1)}, u32[]{:S(2)}, u32[]{:S(2)}) collective-permute-start(f32[16,2,32,128]{3,2,1,0:T(8,128)} %get-tuple-element.39), channel_id=1, source_target_pairs={{0,1},{1,2},{2,3},{3,4},{4,5},{5,6},{6,7},{7,0},{8,9},{9,10},{10,1... | collective-permute-start | bytes 1572872 | tf_op jit(solution)/shard_map/ppermute | solution.py:34
  5.8 16.1 %collective-permute-start.1 = (f32[16,2,32,128]{3,2,1,0:T(8,128)}, f32[16,2,32,128]{3,2,1,0:T(8,128)S(1)}, u32[]{:S(2)}, u32[]{:S(2)}) collective-permute-start(f32[16,2,32,128]{3,2,1,0:T(8,128)} %get-tuple-element.40), channel_id=1, source_target_pairs={{0,7},{1,0},{2,1},{3,2},{4,3},{5,4},{6,5},{7,6},{8,15},{9,8},{10,9... | collective-permute-start | bytes 1572872 | tf_op jit(solution)/shard_map/ppermute | solution.py:34
  9.4 12.5 %collective-permute-start.2 = (f32[22,32,128]{2,1,0:T(8,128)}, f32[22,32,128]{2,1,0:T(8,128)S(1)}, u32[]{:S(2)}, u32[]{:S(2)}) collective-permute-start(f32[22,32,128]{2,1,0:T(8,128)} %get-tuple-element.41), channel_id=1, source_target_pairs={{0,8},{1,9},{2,10},{3,11},{4,12},{5,13},{6,14},{7,15},{8,16},{9,17... | collective-permute-start | bytes 1081352 | tf_op jit(solution)/shard_map/ppermute | solution.py:34
  11.0 11.0 %collective-permute-start.3 = (f32[22,32,128]{2,1,0:T(8,128)}, f32[22,32,128]{2,1,0:T(8,128)S(1)}, u32[]{:S(2)}, u32[]{:S(2)}) collective-permute-start(f32[22,32,128]{2,1,0:T(8,128)} %get-tuple-element.42), channel_id=1, source_target_pairs={{0,120},{1,121},{2,122},{3,123},{4,124},{5,125},{6,126},{7,127},{8... | collective-permute-start | bytes 1081352 | tf_op jit(solution)/shard_map/ppermute | solution.py:34
  21.9 10.1 %copy-start.5 = (f32[22,32,128]{2,1,0:T(8,128)}, f32[22,32,128]{2,1,0:T(8,128)S(1)}, u32[]{:S(2)}) copy-start(f32[22,32,128]{2,1,0:T(8,128)S(1)} %collective-permute-done.2.wide_low) | copy-start | bytes 1081348
  21.9 10.1 %copy-start.6 = (f32[22,32,128]{2,1,0:T(8,128)}, f32[22,32,128]{2,1,0:T(8,128)S(1)}, u32[]{:S(2)}) copy-start(f32[22,32,128]{2,1,0:T(8,128)S(1)} %collective-permute-done.3.wide_high) | copy-start | bytes 1081348
  21.9 10.1 %copy-start.1 = (f32[16,2,32,128]{3,2,1,0:T(8,128)}, f32[16,2,32,128]{3,2,1,0:T(8,128)S(1)}, u32[]{:S(2)}) copy-start(f32[16,2,32,128]{3,2,1,0:T(8,128)S(1)} %collective-permute-done.side_low) | copy-start | bytes 1572868
  22.0 10.1 %copy-start.2 = (f32[16,2,32,128]{3,2,1,0:T(8,128)}, f32[16,2,32,128]{3,2,1,0:T(8,128)S(1)}, u32[]{:S(2)}) copy-start(f32[16,2,32,128]{3,2,1,0:T(8,128)S(1)} %collective-permute-done.1.side_high) | copy-start | bytes 1572868
  22.0 25.9 %all-to-all-start = ((f32[128,1,1408]{2,1,0:T(1,128)}), f32[128,1,1408]{2,1,0:T(1,128)S(1)}, u32[]{:S(2)}, u32[]{:S(2)}) async-start(f32[128,1,1408]{2,1,0:T(1,128)} %shard_map.105), calls=%async_computation | async-start | bytes 1441792 | tf_op jit(solution)/shard_map/all_to_all | solution.py:657
  47.8 8.3 %copy-start = (f32[128,1,1408]{2,1,0:T(1,128)}, f32[128,1,1408]{2,1,0:T(1,128)S(1)}, u32[]{:S(2)}) copy-start(f32[128,1,1408]{2,1,0:T(1,128)S(1)} %all-to-all-done.got_any.got) | copy-start | bytes 2162692
  47.9 19.6 %collective-permute-start.6 = (f32[16,3,32,128]{3,2,1,0:T(8,128)}, f32[16,3,32,128]{3,2,1,0:T(8,128)S(1)}, u32[]{:S(2)}, u32[]{:S(2)}) collective-permute-start(f32[16,3,32,128]{3,2,1,0:T(8,128)} %get-tuple-element.59), channel_id=1, source_target_pairs={{0,1},{1,2},{2,3},{3,4},{4,5},{5,6},{6,7},{7,0},{8,9},{9,10},{10,1... | collective-permute-start | bytes 2359304 | tf_op jit(solution)/shard_map/ppermute | solution.py:34
  47.9 19.6 %collective-permute-start.7 = (f32[16,3,32,128]{3,2,1,0:T(8,128)}, f32[16,3,32,128]{3,2,1,0:T(8,128)S(1)}, u32[]{:S(2)}, u32[]{:S(2)}) collective-permute-start(f32[16,3,32,128]{3,2,1,0:T(8,128)} %get-tuple-element.60), channel_id=1, source_target_pairs={{0,7},{1,0},{2,1},{3,2},{4,3},{5,4},{6,5},{7,6},{8,15},{9,8},{10,9... | collective-permute-start | bytes 2359304 | tf_op jit(solution)/shard_map/ppermute | solution.py:34
  50.8 31.1 %collective-permute-start.4 = (f32[3,16,32,128]{3,2,1,0:T(8,128)}, f32[3,16,32,128]{3,2,1,0:T(8,128)S(1)}, u32[]{:S(2)}, u32[]{:S(2)}) collective-permute-start(f32[3,16,32,128]{3,2,1,0:T(8,128)} %get-tuple-element.56), channel_id=1, source_target_pairs={{0,8},{1,9},{2,10},{3,11},{4,12},{5,13},{6,14},{7,15},{8,16},{9,17... | collective-permute-start | bytes 2359304 | tf_op jit(solution)/shard_map/ppermute | solution.py:34
  51.4 30.5 %collective-permute-start.5 = (f32[3,16,32,128]{3,2,1,0:T(8,128)}, f32[3,16,32,128]{3,2,1,0:T(8,128)S(1)}, u32[]{:S(2)}, u32[]{:S(2)}) collective-permute-start(f32[3,16,32,128]{3,2,1,0:T(8,128)} %get-tuple-element.57), channel_id=1, source_target_pairs={{0,120},{1,121},{2,122},{3,123},{4,124},{5,125},{6,126},{7,127},{8... | collective-permute-start | bytes 2359304 | tf_op jit(solution)/shard_map/ppermute | solution.py:34
  67.4 5.7 %copy-start.3 = (f32[16,3,32,128]{3,2,1,0:T(8,128)}, f32[16,3,32,128]{3,2,1,0:T(8,128)S(1)}, u32[]{:S(2)}) copy-start(f32[16,3,32,128]{3,2,1,0:T(8,128)S(1)} %collective-permute-done.6.aside_low) | copy-start | bytes 2359300
  67.4 5.6 %copy-start.4 = (f32[16,3,32,128]{3,2,1,0:T(8,128)}, f32[16,3,32,128]{3,2,1,0:T(8,128)S(1)}, u32[]{:S(2)}) copy-start(f32[16,3,32,128]{3,2,1,0:T(8,128)S(1)} %collective-permute-done.7.aside_high) | copy-start | bytes 2359300
  68.5 1.6 %collective-permute-start.9 = (f32[16,3,128]{2,1,0:T(4,128)S(1)}, f32[16,3,128]{2,1,0:T(4,128)S(1)}, u32[]{:S(2)}, u32[]{:S(2)}) collective-permute-start(f32[16,3,128]{2,1,0:T(4,128)S(1)} %get-tuple-element.66), channel_id=1, source_target_pairs={{0,7},{1,0},{2,1},{3,2},{4,3},{5,4},{6,5},{7,6},{8,15},{9,8},{10,9... | collective-permute-start | bytes 73736 | tf_op jit(solution)/shard_map/ppermute | solution.py:34
  68.5 4.6 %collective-permute-start.8 = (f32[16,3,128]{2,1,0:T(4,128)S(1)}, f32[16,3,128]{2,1,0:T(4,128)S(1)}, u32[]{:S(2)}, u32[]{:S(2)}) collective-permute-start(f32[16,3,128]{2,1,0:T(4,128)S(1)} %get-tuple-element.67), channel_id=1, source_target_pairs={{0,1},{1,2},{2,3},{3,4},{4,5},{5,6},{6,7},{7,0},{8,9},{9,10},{10,1... | collective-permute-start | bytes 73736 | tf_op jit(solution)/shard_map/ppermute | solution.py:34
  70.1 3.0 %copy-start.11 = (f32[16,3,128]{2,1,0:T(4,128)}, f32[16,3,128]{2,1,0:T(4,128)S(1)}, u32[]{:S(2)}) copy-start(f32[16,3,128]{2,1,0:T(4,128)S(1)} %collective-permute-done.9.beside_high) | copy-start | bytes 73732
  73.1 0.6 copy-start.12
  76.4 9.4 %collective-permute-start.10 = (f32[13,32,128]{2,1,0:T(8,128)}, f32[13,32,128]{2,1,0:T(8,128)S(1)}, u32[]{:S(2)}, u32[]{:S(2)}) collective-permute-start(f32[13,32,128]{2,1,0:T(8,128)} %get-tuple-element.64), channel_id=1, source_target_pairs={{0,8},{1,9},{2,10},{3,11},{4,12},{5,13},{6,14},{7,15},{8,16},{9,17... | collective-permute-start | bytes 638984 | tf_op jit(solution)/shard_map/ppermute | solution.py:34
  76.5 9.4 %collective-permute-start.11 = (f32[13,32,128]{2,1,0:T(8,128)}, f32[13,32,128]{2,1,0:T(8,128)S(1)}, u32[]{:S(2)}, u32[]{:S(2)}) collective-permute-start(f32[13,32,128]{2,1,0:T(8,128)} %get-tuple-element.65), channel_id=1, source_target_pairs={{0,120},{1,121},{2,122},{3,123},{4,124},{5,125},{6,126},{7,127},{8... | collective-permute-start | bytes 638984 | tf_op jit(solution)/shard_map/ppermute | solution.py:34
  81.9 4.0 %copy-start.7 = (f32[3,16,32,128]{3,2,1,0:T(8,128)}, f32[3,16,32,128]{3,2,1,0:T(8,128)S(1)}, u32[]{:S(2)}) copy-start(f32[3,16,32,128]{3,2,1,0:T(8,128)S(1)} %collective-permute-done.4.out_low) | copy-start | bytes 2359300
  81.9 4.0 %copy-start.8 = (f32[3,16,32,128]{3,2,1,0:T(8,128)}, f32[3,16,32,128]{3,2,1,0:T(8,128)S(1)}, u32[]{:S(2)}) copy-start(f32[3,16,32,128]{3,2,1,0:T(8,128)S(1)} %collective-permute-done.5.out_high) | copy-start | bytes 2359300
  85.9 0.7 copy-start.9
  86.6 0.7 copy-start.10
